TPU v7x, 256 devices: a whole 4x4x8 slice. The times are simulated.
256 devices in a mesh: gx: 4 (over x), gy: 8 (over z_lo, core), gz: 8 (over z_hi, y).
Axes of the slice: x: 4, y: 4, z: 8 (z_hi: 2, z_lo: 4; z = z_hi * 4 + z_lo), core: 2. Of those that a mesh axis runs over, the one named last changes fastest.
Arguments:
- populations: float32 [1024, 19, 4096], P(('gx', 'gy', 'gz')), as said below
- neighbours: int32 [1024, 6], P(('gx', 'gy', 'gz')), may hold values from -1 to 1023, as said below
- substeps: int32 [1024], P(('gx', 'gy', 'gz')), may hold values from 1 to 4
- moves: int32 [256, 2], P(('gx', 'gy', 'gz')), may hold values from 0 to 3, as said below
Outputs:
- new_populations: float32 [1024, 19, 4096], P(('gx', 'gy', 'gz'))
- block_ids: int32 [1024], P(('gx', 'gy', 'gz'))
Inputs may be any that keep to these rules, and one draw needn't show every extreme that they name: `neighbours`: each entry is -1 or a block whose index differs from the block's own by at most 4. `moves`: each row holds 2 different slots. `populations`: every population is positive.
All inputs are finite; a program needn't handle non-finite values.
Results may differ from a plain program's by a relative error of at most 0.0003.
Values sent between devices are 32-bit elements; how exact they have to be, the bound alone decides.
A program may use at most 128 MiB of HBM per device.

v0:
```python
import jax
import jax.numpy as jnp
import numpy as np
from jax import lax
from jax.sharding import PartitionSpec as P

BE = 16


VELOCITY = np.array(
    [
        [0, 0, 0],
        [1, 0, 0],
        [-1, 0, 0],
        [0, 1, 0],
        [0, -1, 0],
        [0, 0, 1],
        [0, 0, -1],
        [1, 1, 0],
        [-1, -1, 0],
        [1, -1, 0],
        [-1, 1, 0],
        [1, 0, 1],
        [-1, 0, -1],
        [1, 0, -1],
        [-1, 0, 1],
        [0, 1, 1],
        [0, -1, -1],
        [0, 1, -1],
        [0, -1, 1],
    ],
    np.int32,
)
OPPOSITE = np.array([0, 2, 1, 4, 3, 6, 5, 8, 7, 10, 9, 12, 11, 14, 13, 16, 15, 18, 17], np.int32)
FACE_DIRECTIONS = np.array(
    [
        [2, 8, 10, 12, 14],
        [1, 7, 9, 11, 13],
        [4, 8, 9, 16, 18],
        [3, 7, 10, 15, 17],
        [6, 12, 13, 16, 17],
        [5, 11, 14, 15, 18],
    ],
    np.int32,
)
FACE_PARTNER = np.array([1, 0, 3, 2, 5, 4], np.int32)
RELAX_FIXED = np.array(
    [0, 1.19, 1.4, 0, 1.2, 0, 1.2, 0, 1.2, 0, 1.4, 0, 1.4, 0, 0, 0, 1.98, 1.98, 1.98], np.float32
)
SHEAR_ROWS = np.array([0, 0, 0, 0, 0, 0, 0, 0, 0, 1, 0, 1, 0, 1, 1, 1, 0, 0, 0], np.float32)
BASE_RATE = 1.6


def passed_along(x, axis, by):
    peers = lax.axis_size(axis)
    pairs = [(i, i + by) for i in range(peers) if 0 <= i + by < peers]
    return lax.ppermute(x, axis, pairs)


def swapped(value, axis, bit):
    mask = 2**bit
    pairs = [(source, source ^ mask) for source in range(lax.axis_size(axis))]
    return lax.ppermute(value, axis, pairs)


def moment_table():
    vel_x, vel_y, vel_z = [VELOCITY[:, k].astype(np.float32) for k in range(3)]
    speed_sq = vel_x**2 + vel_y**2 + vel_z**2
    moment_list = [
        np.ones(19, np.float32),
        19 * speed_sq - 30,
        (21 * speed_sq**2 - 53 * speed_sq + 24) / 2,
        vel_x,
        (5 * speed_sq - 9) * vel_x,
        vel_y,
        (5 * speed_sq - 9) * vel_y,
        vel_z,
        (5 * speed_sq - 9) * vel_z,
        3 * vel_x**2 - speed_sq,
        (3 * speed_sq - 5) * (3 * vel_x**2 - speed_sq),
        vel_y**2 - vel_z**2,
        (3 * speed_sq - 5) * (vel_y**2 - vel_z**2),
        vel_x * vel_y,
        vel_y * vel_z,
        vel_x * vel_z,
        (vel_y**2 - vel_z**2) * vel_x,
        (vel_z**2 - vel_x**2) * vel_y,
        (vel_x**2 - vel_y**2) * vel_z,
    ]
    return np.stack(moment_list).astype(np.float32)


def inverse_table():
    table = moment_table()
    return (table.T / (table**2).sum(1)).astype(np.float32)


def build_masks(block_edge):
    flat = np.arange(block_edge**3, dtype=np.int32)
    positions = np.stack(
        [flat // (block_edge * block_edge), flat // block_edge % block_edge, flat % block_edge]
    )
    result = np.zeros((6, 19, block_edge**3), np.int32)
    for which in range(19):
        source = positions - VELOCITY[which][:, None]
        settled = np.zeros(block_edge**3, bool)
        for axis_num in range(3):
            below = (source[axis_num] < 0) & ~settled
            beyond = (source[axis_num] > block_edge - 1) & ~settled
            result[2 * axis_num, which, below] = 1
            result[2 * axis_num + 1, which, beyond] = 1
            settled = settled | below | beyond
    return result


def face_pack(state):
    block_cube = state.reshape(19, BE, BE, BE)
    faces = [
        block_cube[:, 0],
        block_cube[:, BE - 1],
        block_cube[:, :, 0],
        block_cube[:, :, BE - 1],
        block_cube[:, :, :, 0],
        block_cube[:, :, :, BE - 1],
    ]
    return jnp.stack([faces[face][FACE_DIRECTIONS[face]].reshape(5, BE * BE) for face in range(6)])


def collide(state, shear_rate):
    moments = jnp.dot(jnp.asarray(moment_table()), state, precision=lax.Precision.HIGHEST)
    density = moments[0]
    flux_x, flux_y, flux_z = (moments[3], moments[5], moments[7])
    flux_sq = flux_x * flux_x + flux_y * flux_y + flux_z * flux_z
    stress_xx = 3 * flux_x * flux_x - flux_sq
    stress_ww = flux_y * flux_y - flux_z * flux_z
    zeros = jnp.zeros_like(density)
    balance = jnp.stack(
        [
            density,
            -11 * density + 19 * flux_sq,
            3 * density - 5.5 * flux_sq,
            flux_x,
            -2.0 / 3.0 * flux_x,
            flux_y,
            -2.0 / 3.0 * flux_y,
            flux_z,
            -2.0 / 3.0 * flux_z,
            stress_xx,
            -0.5 * stress_xx,
            stress_ww,
            -0.5 * stress_ww,
            flux_x * flux_y,
            flux_y * flux_z,
            flux_x * flux_z,
            zeros,
            zeros,
            zeros,
        ]
    )
    relax_rates = RELAX_FIXED[:, None] + SHEAR_ROWS[:, None] * shear_rate
    relaxed = moments - relax_rates * (moments - balance)
    return jnp.dot(jnp.asarray(inverse_table()), relaxed, precision=lax.Precision.HIGHEST)


def face_plane(halo_in, face):
    return (
        jnp.zeros((19, BE, BE), halo_in.dtype)
        .at[FACE_DIRECTIONS[face ^ 1]]
        .set(halo_in[face].reshape(5, BE, BE))
    )


def stream(post, halo_in, wall_faces):
    extended = jnp.pad(post.reshape(19, BE, BE, BE), ((0, 0), (1, 1), (1, 1), (1, 1)))
    extended = extended.at[:, 1:-1, 1:-1, 0].set(face_plane(halo_in, 4))
    extended = extended.at[:, 1:-1, 1:-1, -1].set(face_plane(halo_in, 5))
    extended = extended.at[:, 1:-1, 0, :].set(
        jnp.pad(face_plane(halo_in, 2), ((0, 0), (0, 0), (1, 1)), mode="edge")
    )
    extended = extended.at[:, 1:-1, -1, :].set(
        jnp.pad(face_plane(halo_in, 3), ((0, 0), (0, 0), (1, 1)), mode="edge")
    )
    extended = extended.at[:, 0, :, :].set(
        jnp.pad(face_plane(halo_in, 0), ((0, 0), (1, 1), (1, 1)), mode="edge")
    )
    extended = extended.at[:, -1, :, :].set(
        jnp.pad(face_plane(halo_in, 1), ((0, 0), (1, 1), (1, 1)), mode="edge")
    )
    moved = []
    for which in range(19):
        step_x, step_y, step_z = [int(v) for v in VELOCITY[which]]
        moved.append(
            extended[
                which,
                1 - step_x : 1 - step_x + BE,
                1 - step_y : 1 - step_y + BE,
                1 - step_z : 1 - step_z + BE,
            ]
        )
    read = jnp.stack(moved).reshape(19, BE**3)
    bounce = jnp.tensordot(wall_faces, jnp.asarray(build_masks(BE)), axes=1) > 0
    return jnp.where(bounce, post[OPPOSITE], read)


def advance(packed):
    state, halo_in, wall_faces, step_count = packed
    shear_rate = 1.0 / (step_count.astype(jnp.float32) * (1.0 / BASE_RATE - 0.5) + 0.5)

    def cycle(index, current):
        return stream(collide(current, shear_rate), halo_in, wall_faces)

    return lax.fori_loop(0, step_count, cycle, state)


def shards(populations, neighbours, substeps, moves):
    blocks = populations.shape[0]
    device_index = lax.axis_index(("gx", "gy", "gz"))
    packed = jax.vmap(face_pack)(populations).reshape(blocks, 30, BE * BE)
    from_before = passed_along(packed, ("gx", "gy", "gz"), 1)
    from_later = passed_along(packed, ("gx", "gy", "gz"), -1)
    candidates = jnp.concatenate([from_before, packed, from_later], axis=0).reshape(
        3 * blocks, 6, 5, BE * BE
    )
    valid = neighbours >= 0
    local_index = jnp.where(valid, neighbours - (device_index - 1) * blocks, blocks)
    halo_in = candidates[local_index, jnp.asarray(FACE_PARTNER)[None, :]]
    halo_in = jnp.where(valid[:, :, None, None], halo_in, 0.0)
    wall_faces = (~valid).astype(jnp.int32)
    block_ids = device_index * blocks + jnp.arange(blocks, dtype=jnp.int32)
    moved_slots = moves[0]
    partner_bit = (lax.axis_size("gy") * lax.axis_size("gz")).bit_length() - 1
    stepped = lax.map(advance, (populations, halo_in, wall_faces, substeps))
    received = swapped(
        (stepped[moved_slots], block_ids[moved_slots]), ("gx", "gy", "gz"), partner_bit
    )
    result = stepped.at[moved_slots].set(received[0])
    block_ids = block_ids.at[moved_slots].set(received[1])
    return (result, block_ids)


def solution(mesh):
    placed = (
        P(("gx", "gy", "gz"), None, None),
        P(("gx", "gy", "gz"), None),
        P(("gx", "gy", "gz")),
        P(("gx", "gy", "gz"), None),
    )
    return jax.shard_map(
        shards,
        mesh=mesh,
        in_specs=placed,
        out_specs=(P(("gx", "gy", "gz"), None, None), P(("gx", "gy", "gz"))),
        check_vma=False,
    )
```

profile of v0, /device:TPU:32, one launch (start us, length us, event | category | flops | bytes accessed | tf_op | source)
XLA Modules:
  0.0 2247.8 jit_solution(2572087190051433336)
XLA Ops:
  0.6 6.9 reshape.605
  14.2 12.4 fusion.21
  30.7 9.1 copy.115
  40.5 9.1 copy.116
  55.3 8.1 collective-permute-start.1
  70.9 2154.4 %while.49 = (s32[]{:T(128)}, f32[4,19,4096]{2,1,0:T(8,128)}, f32[4,19,4096]{2,0,1:T(4,128)}, s32[4]{0:T(128)}, f32[4,6,5,256]{3,2,1,0:T(8,128)}, /*index=5*/s32[...) while((s32[]{:T(128)}, f32[4,19,4096]{2,1,0:T(8,128)}, ...), condition=%wide.region_9.10_spmd.clone.clone, body=%wide.region_0.9_spmd.sunk.clone.clone.sunk | while | flops 36999056 | bytes 17585180 | solution.py:232
  81.6 5.6 fusion.45
  91.9 517.0 %while.50 = (s32[]{:T(128)}, f32[19,4096]{1,0:T(8,128)S(1)}, s32[]{:T(128)}, s32[19,4096]{1,0:T(8,128)}, f32[]{:T(128)}, /*index=5*/f32[19,16,16]{0,2,1:T(8,128)...) while((s32[]{:T(128)}, f32[19,4096]{1,0:T(8,128)S(1)}, ...), condition=%wide.region_8.8_spmd.clone, body=%wide.region_7.7_spmd.sunk.clone.sunk | while | flops 35972136 | bytes 11495313 | solution.py:212
  101.6 19.5 scatter.192
  124.6 60.9 %scatter.193 = f32[19,18,18,18]{3,2,1,0:T(8,128)} dynamic-update-slice(f32[19,18,18,18]{3,2,1,0:T(8,128)} %scatter.192, f32[19,16,16,1]{3,2,1,0:T(8,128)S(1)} %copy.139, s32[]{:T(128)} %constant.452.clone.1..sunk.1..sunk, s32[]{:T(128)} %constant.444.clone.4..sunk.1..sunk, s32[]{:T(128)} %constant.444.clone.4..sunk.1..sunk, s32[]{:T(128)} %constant.443.clone.7..sunk2) | dynamic-update-slice | bytes 38916 | tf_op jit(solution)/shard_map/while/body/eval_jaxpr/while/body/scatter | solution.py:176
  230.7 19.5 scatter.192
  253.7 60.9 %scatter.193 = f32[19,18,18,18]{3,2,1,0:T(8,128)} dynamic-update-slice(f32[19,18,18,18]{3,2,1,0:T(8,128)} %scatter.192, f32[19,16,16,1]{3,2,1,0:T(8,128)S(1)} %copy.139, s32[]{:T(128)} %constant.452.clone.1..sunk.1..sunk, s32[]{:T(128)} %constant.444.clone.4..sunk.1..sunk, s32[]{:T(128)} %constant.444.clone.4..sunk.1..sunk, s32[]{:T(128)} %constant.443.clone.7..sunk2) | dynamic-update-slice | bytes 38916 | tf_op jit(solution)/shard_map/while/body/eval_jaxpr/while/body/scatter | solution.py:176
  320.2 5.5 scatter.195
  359.8 19.5 scatter.192
  382.8 60.9 %scatter.193 = f32[19,18,18,18]{3,2,1,0:T(8,128)} dynamic-update-slice(f32[19,18,18,18]{3,2,1,0:T(8,128)} %scatter.192, f32[19,16,16,1]{3,2,1,0:T(8,128)S(1)} %copy.139, s32[]{:T(128)} %constant.452.clone.1..sunk.1..sunk, s32[]{:T(128)} %constant.444.clone.4..sunk.1..sunk, s32[]{:T(128)} %constant.444.clone.4..sunk.1..sunk, s32[]{:T(128)} %constant.443.clone.7..sunk2) | dynamic-update-slice | bytes 38916 | tf_op jit(solution)/shard_map/while/body/eval_jaxpr/while/body/scatter | solution.py:176
  488.9 19.5 scatter.192
  511.9 60.9 %scatter.193 = f32[19,18,18,18]{3,2,1,0:T(8,128)} dynamic-update-slice(f32[19,18,18,18]{3,2,1,0:T(8,128)} %scatter.192, f32[19,16,16,1]{3,2,1,0:T(8,128)S(1)} %copy.139, s32[]{:T(128)} %constant.452.clone.1..sunk.1..sunk, s32[]{:T(128)} %constant.444.clone.4..sunk.1..sunk, s32[]{:T(128)} %constant.444.clone.4..sunk.1..sunk, s32[]{:T(128)} %constant.443.clone.7..sunk2) | dynamic-update-slice | bytes 38916 | tf_op jit(solution)/shard_map/while/body/eval_jaxpr/while/body/scatter | solution.py:176
  620.2 5.6 fusion.45
  630.4 517.0 %while.50 = (s32[]{:T(128)}, f32[19,4096]{1,0:T(8,128)S(1)}, s32[]{:T(128)}, s32[19,4096]{1,0:T(8,128)}, f32[]{:T(128)}, /*index=5*/f32[19,16,16]{0,2,1:T(8,128)...) while((s32[]{:T(128)}, f32[19,4096]{1,0:T(8,128)S(1)}, ...), condition=%wide.region_8.8_spmd.clone, body=%wide.region_7.7_spmd.sunk.clone.sunk | while | flops 35972136 | bytes 11495313 | solution.py:212
  640.2 19.5 scatter.192
  663.2 60.9 %scatter.193 = f32[19,18,18,18]{3,2,1,0:T(8,128)} dynamic-update-slice(f32[19,18,18,18]{3,2,1,0:T(8,128)} %scatter.192, f32[19,16,16,1]{3,2,1,0:T(8,128)S(1)} %copy.139, s32[]{:T(128)} %constant.452.clone.1..sunk.1..sunk, s32[]{:T(128)} %constant.444.clone.4..sunk.1..sunk, s32[]{:T(128)} %constant.444.clone.4..sunk.1..sunk, s32[]{:T(128)} %constant.443.clone.7..sunk2) | dynamic-update-slice | bytes 38916 | tf_op jit(solution)/shard_map/while/body/eval_jaxpr/while/body/scatter | solution.py:176
  769.3 19.5 scatter.192
  792.3 60.9 %scatter.193 = f32[19,18,18,18]{3,2,1,0:T(8,128)} dynamic-update-slice(f32[19,18,18,18]{3,2,1,0:T(8,128)} %scatter.192, f32[19,16,16,1]{3,2,1,0:T(8,128)S(1)} %copy.139, s32[]{:T(128)} %constant.452.clone.1..sunk.1..sunk, s32[]{:T(128)} %constant.444.clone.4..sunk.1..sunk, s32[]{:T(128)} %constant.444.clone.4..sunk.1..sunk, s32[]{:T(128)} %constant.443.clone.7..sunk2) | dynamic-update-slice | bytes 38916 | tf_op jit(solution)/shard_map/while/body/eval_jaxpr/while/body/scatter | solution.py:176
  898.3 19.5 scatter.192
  921.4 60.9 %scatter.193 = f32[19,18,18,18]{3,2,1,0:T(8,128)} dynamic-update-slice(f32[19,18,18,18]{3,2,1,0:T(8,128)} %scatter.192, f32[19,16,16,1]{3,2,1,0:T(8,128)S(1)} %copy.139, s32[]{:T(128)} %constant.452.clone.1..sunk.1..sunk, s32[]{:T(128)} %constant.444.clone.4..sunk.1..sunk, s32[]{:T(128)} %constant.444.clone.4..sunk.1..sunk, s32[]{:T(128)} %constant.443.clone.7..sunk2) | dynamic-update-slice | bytes 38916 | tf_op jit(solution)/shard_map/while/body/eval_jaxpr/while/body/scatter | solution.py:176
  1027.4 19.5 scatter.192
  1050.4 60.9 %scatter.193 = f32[19,18,18,18]{3,2,1,0:T(8,128)} dynamic-update-slice(f32[19,18,18,18]{3,2,1,0:T(8,128)} %scatter.192, f32[19,16,16,1]{3,2,1,0:T(8,128)S(1)} %copy.139, s32[]{:T(128)} %constant.452.clone.1..sunk.1..sunk, s32[]{:T(128)} %constant.444.clone.4..sunk.1..sunk, s32[]{:T(128)} %constant.444.clone.4..sunk.1..sunk, s32[]{:T(128)} %constant.443.clone.7..sunk2) | dynamic-update-slice | bytes 38916 | tf_op jit(solution)/shard_map/while/body/eval_jaxpr/while/body/scatter | solution.py:176
  1158.7 5.6 fusion.45
  1169.0 517.0 %while.50 = (s32[]{:T(128)}, f32[19,4096]{1,0:T(8,128)S(1)}, s32[]{:T(128)}, s32[19,4096]{1,0:T(8,128)}, f32[]{:T(128)}, /*index=5*/f32[19,16,16]{0,2,1:T(8,128)...) while((s32[]{:T(128)}, f32[19,4096]{1,0:T(8,128)S(1)}, ...), condition=%wide.region_8.8_spmd.clone, body=%wide.region_7.7_spmd.sunk.clone.sunk | while | flops 35972136 | bytes 11495313 | solution.py:212
  1178.7 19.5 scatter.192
  1201.7 60.9 %scatter.193 = f32[19,18,18,18]{3,2,1,0:T(8,128)} dynamic-update-slice(f32[19,18,18,18]{3,2,1,0:T(8,128)} %scatter.192, f32[19,16,16,1]{3,2,1,0:T(8,128)S(1)} %copy.139, s32[]{:T(128)} %constant.452.clone.1..sunk.1..sunk, s32[]{:T(128)} %constant.444.clone.4..sunk.1..sunk, s32[]{:T(128)} %constant.444.clone.4..sunk.1..sunk, s32[]{:T(128)} %constant.443.clone.7..sunk2) | dynamic-update-slice | bytes 38916 | tf_op jit(solution)/shard_map/while/body/eval_jaxpr/while/body/scatter | solution.py:176
  1307.8 19.5 scatter.192
  1330.8 60.9 %scatter.193 = f32[19,18,18,18]{3,2,1,0:T(8,128)} dynamic-update-slice(f32[19,18,18,18]{3,2,1,0:T(8,128)} %scatter.192, f32[19,16,16,1]{3,2,1,0:T(8,128)S(1)} %copy.139, s32[]{:T(128)} %constant.452.clone.1..sunk.1..sunk, s32[]{:T(128)} %constant.444.clone.4..sunk.1..sunk, s32[]{:T(128)} %constant.444.clone.4..sunk.1..sunk, s32[]{:T(128)} %constant.443.clone.7..sunk2) | dynamic-update-slice | bytes 38916 | tf_op jit(solution)/shard_map/while/body/eval_jaxpr/while/body/scatter | solution.py:176
  1436.9 19.5 scatter.192
  1459.9 60.9 %scatter.193 = f32[19,18,18,18]{3,2,1,0:T(8,128)} dynamic-update-slice(f32[19,18,18,18]{3,2,1,0:T(8,128)} %scatter.192, f32[19,16,16,1]{3,2,1,0:T(8,128)S(1)} %copy.139, s32[]{:T(128)} %constant.452.clone.1..sunk.1..sunk, s32[]{:T(128)} %constant.444.clone.4..sunk.1..sunk, s32[]{:T(128)} %constant.444.clone.4..sunk.1..sunk, s32[]{:T(128)} %constant.443.clone.7..sunk2) | dynamic-update-slice | bytes 38916 | tf_op jit(solution)/shard_map/while/body/eval_jaxpr/while/body/scatter | solution.py:176
  1566.0 19.5 scatter.192
  1589.0 60.9 %scatter.193 = f32[19,18,18,18]{3,2,1,0:T(8,128)} dynamic-update-slice(f32[19,18,18,18]{3,2,1,0:T(8,128)} %scatter.192, f32[19,16,16,1]{3,2,1,0:T(8,128)S(1)} %copy.139, s32[]{:T(128)} %constant.452.clone.1..sunk.1..sunk, s32[]{:T(128)} %constant.444.clone.4..sunk.1..sunk, s32[]{:T(128)} %constant.444.clone.4..sunk.1..sunk, s32[]{:T(128)} %constant.443.clone.7..sunk2) | dynamic-update-slice | bytes 38916 | tf_op jit(solution)/shard_map/while/body/eval_jaxpr/while/body/scatter | solution.py:176
  1697.2 5.6 fusion.45
  1707.5 517.0 %while.50 = (s32[]{:T(128)}, f32[19,4096]{1,0:T(8,128)S(1)}, s32[]{:T(128)}, s32[19,4096]{1,0:T(8,128)}, f32[]{:T(128)}, /*index=5*/f32[19,16,16]{0,2,1:T(8,128)...) while((s32[]{:T(128)}, f32[19,4096]{1,0:T(8,128)S(1)}, ...), condition=%wide.region_8.8_spmd.clone, body=%wide.region_7.7_spmd.sunk.clone.sunk | while | flops 35972136 | bytes 11495313 | solution.py:212
  1717.3 19.5 scatter.192
  1740.3 60.9 %scatter.193 = f32[19,18,18,18]{3,2,1,0:T(8,128)} dynamic-update-slice(f32[19,18,18,18]{3,2,1,0:T(8,128)} %scatter.192, f32[19,16,16,1]{3,2,1,0:T(8,128)S(1)} %copy.139, s32[]{:T(128)} %constant.452.clone.1..sunk.1..sunk, s32[]{:T(128)} %constant.444.clone.4..sunk.1..sunk, s32[]{:T(128)} %constant.444.clone.4..sunk.1..sunk, s32[]{:T(128)} %constant.443.clone.7..sunk2) | dynamic-update-slice | bytes 38916 | tf_op jit(solution)/shard_map/while/body/eval_jaxpr/while/body/scatter | solution.py:176
  1846.3 19.5 scatter.192
  1869.3 60.9 %scatter.193 = f32[19,18,18,18]{3,2,1,0:T(8,128)} dynamic-update-slice(f32[19,18,18,18]{3,2,1,0:T(8,128)} %scatter.192, f32[19,16,16,1]{3,2,1,0:T(8,128)S(1)} %copy.139, s32[]{:T(128)} %constant.452.clone.1..sunk.1..sunk, s32[]{:T(128)} %constant.444.clone.4..sunk.1..sunk, s32[]{:T(128)} %constant.444.clone.4..sunk.1..sunk, s32[]{:T(128)} %constant.443.clone.7..sunk2) | dynamic-update-slice | bytes 38916 | tf_op jit(solution)/shard_map/while/body/eval_jaxpr/while/body/scatter | solution.py:176
  1975.4 19.5 scatter.192
  1998.4 60.9 %scatter.193 = f32[19,18,18,18]{3,2,1,0:T(8,128)} dynamic-update-slice(f32[19,18,18,18]{3,2,1,0:T(8,128)} %scatter.192, f32[19,16,16,1]{3,2,1,0:T(8,128)S(1)} %copy.139, s32[]{:T(128)} %constant.452.clone.1..sunk.1..sunk, s32[]{:T(128)} %constant.444.clone.4..sunk.1..sunk, s32[]{:T(128)} %constant.444.clone.4..sunk.1..sunk, s32[]{:T(128)} %constant.443.clone.7..sunk2) | dynamic-update-slice | bytes 38916 | tf_op jit(solution)/shard_map/while/body/eval_jaxpr/while/body/scatter | solution.py:176
  2104.5 19.5 scatter.192
  2127.5 60.9 %scatter.193 = f32[19,18,18,18]{3,2,1,0:T(8,128)} dynamic-update-slice(f32[19,18,18,18]{3,2,1,0:T(8,128)} %scatter.192, f32[19,16,16,1]{3,2,1,0:T(8,128)S(1)} %copy.139, s32[]{:T(128)} %constant.452.clone.1..sunk.1..sunk, s32[]{:T(128)} %constant.444.clone.4..sunk.1..sunk, s32[]{:T(128)} %constant.444.clone.4..sunk.1..sunk, s32[]{:T(128)} %constant.443.clone.7..sunk2) | dynamic-update-slice | bytes 38916 | tf_op jit(solution)/shard_map/while/body/eval_jaxpr/while/body/scatter | solution.py:176
  2230.8 12.3 collective-permute-done.3
  (876 shorter events, 853.6 us)
Async XLA Ops:
  14.1 12.5 copy-start.8
  14.1 12.5 copy-start.9
  40.5 9.1 copy-start.14
  40.5 22.9 %copy-start.10 = (s32[4,6]{1,0:T(4,128)S(1)}, s32[4,6]{1,0:T(4,128)}, u32[]{:S(2)}) copy-start(s32[4,6]{1,0:T(4,128)} %param.53) | copy-start | bytes 292
  40.5 23.5 %copy-start.13 = (s32[6]{0:T(128)S(1)}, s32[6]{0:T(128)}, u32[]{:S(2)}) copy-start(s32[6]{0:T(128)} %constant.527) | copy-start | bytes 76
  49.6 21.3 copy-start.2
  49.6 21.3 copy-start.3
  49.6 21.3 copy-start.5
  49.7 21.2 copy-start.6
  49.7 21.2 copy-start.7
  49.7 1.8 copy-start.11
  51.8 17.5 collective-permute-start
  55.3 14.0 collective-permute-start.1
  219.9 1.0 copy-start.1
  349.0 1.0 copy-start.1
  478.1 1.0 copy-start.1
  607.2 1.0 copy-start.1
  758.5 1.0 copy-start.1
  887.6 1.0 copy-start.1
  1016.6 1.0 copy-start.1
  1145.7 1.0 copy-start.1
  1297.0 1.0 copy-start.1
  1426.1 1.0 copy-start.1
  1555.2 1.0 copy-start.1
  1684.3 1.0 copy-start.1
  1835.6 1.0 copy-start.1
  1964.6 1.0 copy-start.1
  2093.7 1.0 copy-start.1
  2222.8 1.0 copy-start.1
  2225.3 17.9 copy-start.12
  2227.4 17.8 copy-start.4
  2227.9 15.8 collective-permute-start.2
  2228.8 14.3 collective-permute-start.3
  2243.7 4.1 copy-start
where the time goes:
time: 2270 us; the launch traced here: 2250 us
  local copies, waits for them, and re-layouts  2140 us (94%)
  matrix products  38.2 us (2%)
    scatter x16, local copies, waits for them, and re-layouts, stream(): extended = extended.at[:, 1:-1, 1:-1, -1].set(face_plane(halo_in, 5))  975 us
    scatter x16, local copies, waits for them, and re-layouts, stream(): extended = extended.at[:, 1:-1, 1:-1, 0].set(face_plane(halo_in, 4))  312 us
    while x328, local copies, waits for them, and re-layouts  299 us
    another operation x88, local copies, waits for them, and re-layouts  112 us
    scatter x16, local copies, waits for them, and re-layouts, stream(): extended.at[:, 1:-1, -1, :]  88.7 us
    scatter x16, local copies, waits for them, and re-layouts, stream(): extended.at[:, 1:-1, 0, :]  88.2 us
    pad x16, local copies, waits for them, and re-layouts, stream(): jnp.pad(post.reshape(19, BE, BE, BE), ((0, 0), (1, 1), (1, 1), (1, 1)))  48.6 us
  transfers between devices with their start and end apart: 4, of which 2 were waited for; matrix products, arithmetic and copies ran while one was open for 0% of the time, Pallas kernels for 0%

commit v1 on v0

v1 whole, which is shorter than its diff:
```python
import functools

import jax
import jax.numpy as jnp
import numpy as np
from jax import lax
from jax.experimental import pallas as pl
from jax.experimental.pallas import tpu as pltpu
from jax.sharding import PartitionSpec as P

MESH = pl.DeviceIdType.MESH
AXES = ("gx", "gy", "gz")
VELOCITY = [
    (0, 0, 0), (1, 0, 0), (-1, 0, 0), (0, 1, 0), (0, -1, 0), (0, 0, 1), (0, 0, -1),
    (1, 1, 0), (-1, -1, 0), (1, -1, 0), (-1, 1, 0), (1, 0, 1), (-1, 0, -1),
    (1, 0, -1), (-1, 0, 1), (0, 1, 1), (0, -1, -1), (0, 1, -1), (0, -1, 1),
]
OPPOSITE = [0, 2, 1, 4, 3, 6, 5, 8, 7, 10, 9, 12, 11, 14, 13, 16, 15, 18, 17]
LEAVING = [
    [2, 8, 10, 12, 14], [1, 7, 9, 11, 13], [4, 8, 9, 16, 18],
    [3, 7, 10, 15, 17], [6, 12, 13, 16, 17], [5, 11, 14, 15, 18],
]
COUNT_ROW, SLOT_ROW, Y_ROW, Z_ROW, SENT_ROWS, PACKET_ROWS = 20, 21, 24, 56, 88, 96
TOP = 8


def turned(value, by):
    by = by % 128
    return value if by == 0 else pltpu.roll(value, by, 1)


def grid_iotas():
    row = lax.broadcasted_iota(jnp.int32, (8, 128), 0)
    lane = lax.broadcasted_iota(jnp.int32, (8, 128), 1)
    return row, lane


def unpacked(raw, cube, block):
    for group in range(3):
        count = min(8, 19 - 8 * group)
        for part in range(4):
            tile = raw[block, 8 * group : 8 * group + count, 1024 * part : 1024 * (part + 1)]
            tile = tile.reshape(count, 8, 128)
            for k in range(count):
                cube[block, 8 * group + k, TOP + 8 * part : TOP + 8 * part + 8, :] = tile[k]


def pack_faces(cube, packets, block, slot):
    row, lane = grid_iotas()
    even = row % 2 == 0
    for face in range(2):
        start = TOP if face == 0 else TOP + 30
        for k in range(5):
            at = 10 * face + 2 * k
            packets[slot, at : at + 2, :] = cube[block, LEAVING[face][k], start : start + 2, :]
    for v in range(4):
        base = TOP + 8 * v
        kept = jnp.zeros((8, 128), jnp.float32)
        for k in range(5):
            far = cube[block, LEAVING[3][k], base + 1 : base + 9, :]
            near = cube[block, LEAVING[2][k], base - 1 : base + 7, :]
            moved = turned(jnp.where(even, far, near), 16 * (k + 1))
            kept = jnp.where(lane // 16 == jnp.where(even, k, k + 1), moved, kept)
        packets[slot, Y_ROW + 8 * v : Y_ROW + 8 * v + 8, :] = kept
        kept = jnp.zeros((8, 128), jnp.float32)
        for k in range(5):
            near = cube[block, LEAVING[4][k], base : base + 8, :]
            far = cube[block, LEAVING[5][k], base : base + 8, :]
            moved = turned(jnp.where(lane % 16 == 15, far, near), 2 * k + 1)
            kept = jnp.where(lane % 16 // 2 == k, moved, kept)
        packets[slot, Z_ROW + 8 * v : Z_ROW + 8 * v + 8, :] = kept


def assemble(packets, nbr, sub, block, first, out, slot, mark):
    row, lane = grid_iotas()
    at, valid = [], []
    for face in range(6):
        near = nbr[block, face]
        valid.append(jnp.full((8, 128), near, jnp.int32) >= 0)
        at.append(jnp.clip(near - first, 0, 11))
    for face in range(2):
        other = 10 * (face ^ 1)
        for start, rows in ((0, 8), (8, 2)):
            value = packets[at[face], other + start : other + start + rows, :]
            out[slot, 10 * face + start : 10 * face + start + rows, :] = jnp.where(
                valid[face][:rows], value, -1.0
            )
    for v in range(4):
        rows = slice(Y_ROW + 8 * v, Y_ROW + 8 * v + 8)
        even_rows = jnp.where(valid[2], packets[at[2], rows, :], -1.0)
        odd_rows = jnp.where(valid[3], packets[at[3], rows, :], -1.0)
        out[slot, rows, :] = jnp.where(row % 2 == 0, even_rows, odd_rows)
        rows = slice(Z_ROW + 8 * v, Z_ROW + 8 * v + 8)
        low = jnp.where(valid[4], packets[at[4], rows, :], -1.0)
        high = jnp.where(valid[5], packets[at[5], rows, :], -1.0)
        out[slot, rows, :] = jnp.where(lane % 2 == 0, low, high)
    count = jnp.full((1, 128), sub[block], jnp.int32).astype(jnp.float32)
    out[slot, COUNT_ROW : COUNT_ROW + 1, :] = count
    out[slot, SLOT_ROW : SLOT_ROW + 1, :] = jnp.full((1, 128), mark, jnp.int32).astype(jnp.float32)


def outside(which, v):
    row, lane = grid_iotas()
    cx, cy, cz = VELOCITY[which]
    x_mask = y_mask = z_mask = None
    if cx == 1 and v == 0:
        x_mask = row < 2
    if cx == -1 and v == 3:
        x_mask = row >= 6
    if cy == 1:
        y_mask = (row % 2 == 0) & (lane < 16)
    if cy == -1:
        y_mask = (row % 2 == 1) & (lane >= 112)
    if cz == 1:
        z_mask = lane % 16 == 0
    if cz == -1:
        z_mask = lane % 16 == 15
    return x_mask, y_mask, z_mask


def build_halo(face_in, slot, halo):
    row, lane = grid_iotas()
    for which in range(1, 19):
        cx, cy, cz = VELOCITY[which]
        for v in range(4):
            x_mask, y_mask, z_mask = outside(which, v)
            value = None
            if z_mask is not None:
                face = 4 if cz == 1 else 5
                k = LEAVING[face ^ 1].index(which)
                by = 16 * cy - (2 * k + 1) + (-15 if cz == 1 else 15)
                start = Z_ROW + 8 * v - 2 * cx
                value = turned(face_in[slot, start : start + 8, :], by)
                if cy != 0:
                    start = start - cy
                    beside = turned(face_in[slot, start : start + 8, :], by)
                    value = jnp.where(lane < 16 if cy == 1 else lane >= 112, beside, value)
            if y_mask is not None:
                face = 2 if cy == 1 else 3
                k = LEAVING[face ^ 1].index(which)
                by = -16 * k if cy == 1 else 112 - 16 * (k + 1)
                start = Y_ROW + 8 * v - 2 * cx
                plane = face_in[slot, start : start + 8, :]
                line = turned(plane, by)
                if cz != 0:
                    line = jnp.where(lane % 16 == (0 if cz == 1 else 15), line, turned(plane, by + cz))
                value = line if value is None else jnp.where(y_mask, line, value)
            if x_mask is not None:
                face = 0 if cx == 1 else 1
                k = LEAVING[face ^ 1].index(which)
                at = 10 * face + 2 * k
                pair = face_in[slot, at : at + 2, :]
                upper, lower = pair[0:1], pair[1:2]
                if cy == 1:
                    high, low = turned(upper, 16), turned(lower, 16)
                    lane1 = lane[0:1]
                    lower = jnp.where(lane1 < 16, high, low)
                    upper = jnp.where(lane1 < 16, upper, high)
                elif cy == -1:
                    high, low = turned(upper, -16), turned(lower, -16)
                    lane1 = lane[0:1]
                    upper = jnp.where(lane1 >= 112, low, high)
                    lower = jnp.where(lane1 >= 112, lower, low)
                elif cz != 0:
                    edge = lane[0:1] % 16 == (0 if cz == 1 else 15)
                    upper = jnp.where(edge, upper, turned(upper, cz))
                    lower = jnp.where(edge, lower, turned(lower, cz))
                spread = jnp.where(
                    row % 2 == 0,
                    jnp.broadcast_to(upper, (8, 128)),
                    jnp.broadcast_to(lower, (8, 128)),
                )
                value = spread if value is None else jnp.where(x_mask, spread, value)
            if value is not None:
                halo[which, 8 * v : 8 * v + 8, :] = value


def collide(f, shear):
    s = {q: f[q] + f[q + 1] for q in range(1, 19, 2)}
    d = {q: f[q] - f[q + 1] for q in range(1, 19, 2)}
    sx, sy, sz = s[1], s[3], s[5]
    sxy, sxz, syz = s[7] + s[9], s[11] + s[13], s[15] + s[17]
    along = sx + (sy + sz)
    across = sxy + (sxz + syz)
    xa, xb = d[7] + d[9], d[11] + d[13]
    ya, yb = d[15] + d[17], d[7] - d[9]
    za, zb = d[11] - d[13], d[15] - d[17]
    x_sum, y_sum, z_sum = xa + xb, ya + yb, za + zb
    jx, jy, jz = d[1] + x_sum, d[3] + y_sum, d[5] + z_sum
    xx, yy, zz = jx * jx, jy * jy, jz * jz
    yz_sum = yy + zz
    jj = xx + yz_sum
    e1 = (1.19 * 19.0 / 2394.0) * ((across - f[0]) - jj)
    e2 = (1.4 / 252.0) * ((9.0 * f[0] - 7.0 * along) - (2.0 * across - 5.5 * jj))
    qx = (1.2 / 40.0 * 5.0 / 3.0) * (x_sum - 2.0 * d[1])
    qy = (1.2 / 40.0 * 5.0 / 3.0) * (y_sum - 2.0 * d[3])
    qz = (1.2 / 40.0 * 5.0 / 3.0) * (z_sum - 2.0 * d[5])
    axial = (2.0 * sx) - (sy + sz)
    planar = (sxy + sxz) - 2.0 * syz
    stress = 2.0 * xx - yz_sum
    e9 = (shear * (1.0 / 36.0)) * ((axial + planar) - stress)
    e10 = (1.4 / 72.0) * ((planar - 2.0 * axial) + 0.5 * stress)
    axial_w = sy - sz
    planar_w = sxy - sxz
    stress_w = yy - zz
    e11 = (shear * (1.0 / 12.0)) * ((axial_w + planar_w) - stress_w)
    e12 = (1.4 / 24.0) * ((planar_w - 2.0 * axial_w) + 0.5 * stress_w)
    quarter = shear * 0.25
    e13 = quarter * ((s[7] - s[9]) - jx * jy)
    e14 = quarter * ((s[15] - s[17]) - jy * jz)
    e15 = quarter * ((s[11] - s[13]) - jx * jz)
    e16 = (1.98 / 8.0) * (xa - xb)
    e17 = (1.98 / 8.0) * (ya - yb)
    e18 = (1.98 / 8.0) * (za - zb)
    post = [None] * 19
    post[0] = f[0] + (30.0 * e1 - 12.0 * e2)
    base = 11.0 * e1 + 4.0 * e2
    t9 = e9 - 2.0 * e10
    t11 = e11 - 2.0 * e12
    evens = {1: 2.0 * t9 - base, 3: t11 - (t9 + base), 5: -((t11 + t9) + base)}
    base = 8.0 * e1 + e2
    u9 = e9 + e10
    u11 = e11 + e12
    upper, lower, third = base + u9 + u11, base + u9 - u11, base - 2.0 * u9
    evens.update({7: upper + e13, 9: upper - e13, 11: lower + e15, 13: lower - e15, 15: third + e14, 17: third - e14})
    xp, xm = qx + e16, qx - e16
    yp, ym = qy + e17, qy - e17
    zp, zm = qz + e18, qz - e18
    odds = {
        1: -4.0 * qx, 3: -4.0 * qy, 5: -4.0 * qz,
        7: xp + ym, 9: xp - ym, 11: xm + zp, 13: xm - zp, 15: yp + zm, 17: yp - zm,
    }
    for q in range(1, 19, 2):
        post[q] = f[q] - (evens[q] + odds[q])
        post[q + 1] = f[q + 1] - (evens[q] - odds[q])
    return post


def cycle(step, state, slot, post, halo, count, shear):
    _, lane = grid_iotas()
    for v in range(4):
        rows = slice(8 * v, 8 * v + 8)
        values = collide([state[slot, q, rows, :] for q in range(19)], shear)
        for q in range(19):
            post[q, TOP + 8 * v : TOP + 8 * v + 8, :] = values[q]
    active = count > step
    for q in range(19):
        cx, cy, cz = VELOCITY[q]
        for v in range(4):
            rows = slice(8 * v, 8 * v + 8)
            start = TOP + 8 * v - 2 * cx
            value = post[q, start : start + 8, :]
            by = 16 * cy + cz
            if cy != 0:
                beside = post[q, start - cy : start - cy + 8, :]
                value = jnp.where(lane >= 128 - by if cy == 1 else lane < -by, beside, value)
            value = turned(value, by)
            masks = [m for m in outside(q, v) if m is not None]
            if masks:
                edge = halo[q, rows, :]
                bounced = post[OPPOSITE[q], TOP + 8 * v : TOP + 8 * v + 8, :]
                value = jnp.where(
                    functools.reduce(jnp.logical_or, masks), jnp.where(edge < 0.0, bounced, edge), value
                )
            state[slot, q, rows, :] = jnp.where(active, value, state[slot, q, rows, :])


def kernel(
    sizes, pop, nbr, sub, moves, out, ids, raw, cube, packets, gone, interface_out, state, interface, post, halo,
    load_sem, send_sem, recv_sem,
):
    ny, nz, total = sizes
    bit = ny * nz
    me = lax.axis_index("gx") * bit + lax.axis_index("gy") * nz + lax.axis_index("gz")

    def place(d):
        return (d // bit, d // nz % ny, d % nz)

    partner_id = lax.rem(me // bit, 2) * (-2 * bit) + bit + me
    partner = place(partner_id)
    later = place(lax.rem(me + 1, total))
    before = place(lax.rem(me + total - 1, total))

    barrier = pltpu.get_barrier_semaphore()
    for other in (partner, before, later):
        pl.semaphore_signal(barrier, inc=1, device_id=other, device_id_type=MESH)

    loads = [pltpu.make_async_copy(pop.at[b], raw.at[b], load_sem.at[b]) for b in range(4)]
    for load in loads:
        load.start()
    for load in loads:
        load.wait()

    def prepare(b, carry):
        unpacked(raw, cube, b)
        pack_faces(cube, packets, b, b + 4)
        return carry

    lax.fori_loop(0, 4, prepare, 0)

    pl.semaphore_wait(barrier, 3)

    def remote(source, target, number, device):
        return pltpu.make_async_remote_copy(
            src_ref=source,
            dst_ref=target,
            send_sem=send_sem.at[number],
            recv_sem=recv_sem.at[number],
            device_id=device,
            device_id_type=MESH,
        )

    mine = packets.at[pl.ds(4, 4), pl.ds(0, SENT_ROWS)]
    to_later = remote(mine, packets.at[pl.ds(0, 4), pl.ds(0, SENT_ROWS)], 0, later)
    to_before = remote(mine, packets.at[pl.ds(8, 4), pl.ds(0, SENT_ROWS)], 1, before)
    to_later.start()
    to_before.start()

    moved = [moves[0, 0], moves[0, 1]]
    blocks = []
    for k in range(2):
        def take(q, carry, k=k):
            gone[k, q] = cube[moved[k], q, TOP : TOP + 32, :]
            return carry

        lax.fori_loop(0, 19, take, 0)
        copy = remote(gone.at[k], state.at[2 + k], 2 + k, partner)
        copy.start()
        blocks.append(copy)

    to_later.wait_recv()
    to_before.wait_recv()

    first = (me - 1) * 4
    faces = []
    for k in range(2):
        assemble(packets, nbr, sub, moved[k], first, interface_out, k, moved[k])
        copy = remote(interface_out.at[k], interface.at[2 + k], 4 + k, partner)
        copy.start()
        faces.append(copy)

    low = jnp.minimum(moved[0], moved[1])
    high = jnp.maximum(moved[0], moved[1])
    stay0 = jnp.where(low > 0, 0, jnp.where(high > 1, 1, 2))
    stay1 = jnp.minimum(6 - low - high - stay0, 3)

    for j, stay in enumerate((stay0, stay1)):
        assemble(packets, nbr, sub, stay, first, interface, j, stay)

        def keep(q, carry, j=j, stay=stay):
            state[j, q] = cube[stay, q, TOP : TOP + 32, :]
            return carry

        lax.fori_loop(0, 19, keep, 0)

    def job(j, carry):
        for k in range(2):
            @pl.when(j == 2 + k)
            def _(k=k):
                faces[k].wait_recv()
                blocks[k].wait_recv()

        count = jnp.broadcast_to(interface[j, COUNT_ROW : COUNT_ROW + 1, :], (8, 128))
        shear = 1.0 / (count * (1.0 / 1.6 - 0.5) + 0.5)
        build_halo(interface, j, halo)

        def one(step, carry):
            at = jnp.full((8, 128), step, jnp.int32).astype(jnp.float32)
            cycle(at, state, j, post, halo, count, shear)
            return carry

        return lax.fori_loop(0, 4, one, carry)

    lax.fori_loop(0, 4, job, 0)

    for s in range(4):
        source = jnp.where(
            moved[0] == s, 2, jnp.where(moved[1] == s, 3, jnp.where(stay0 == s, 0, 1))
        )
        for group in range(3):
            count = min(8, 19 - 8 * group)
            for part in range(4):
                tile = state[source, 8 * group : 8 * group + count, 8 * part : 8 * part + 8, :]
                out[s, 8 * group : 8 * group + count, 1024 * part : 1024 * (part + 1)] = tile.reshape(count, 1024)

    marks = [
        jnp.max(interface[2 + k, SLOT_ROW : SLOT_ROW + 1, :]).astype(jnp.int32) + partner_id * 4 for k in range(2)
    ]
    for s in range(4):
        ids[s] = jnp.where(moved[0] == s, marks[0], jnp.where(moved[1] == s, marks[1], me * 4 + s))

    to_later.wait_send()
    to_before.wait_send()
    for k in range(2):
        blocks[k].wait_send()
        faces[k].wait_send()


def shards(sizes, populations, neighbours, substeps, moves):
    f32 = jnp.float32
    return pl.pallas_call(
        functools.partial(kernel, sizes),
        out_shape=(jax.ShapeDtypeStruct((4, 19, 4096), f32), jax.ShapeDtypeStruct((4,), jnp.int32)),
        in_specs=[
            pl.BlockSpec(memory_space=pl.ANY),
            pl.BlockSpec(memory_space=pltpu.SMEM),
            pl.BlockSpec(memory_space=pltpu.SMEM),
            pl.BlockSpec(memory_space=pltpu.SMEM),
        ],
        out_specs=(pl.BlockSpec(memory_space=pltpu.VMEM), pl.BlockSpec(memory_space=pltpu.SMEM)),
        scratch_shapes=[
            pltpu.VMEM((4, 19, 4096), f32),
            pltpu.VMEM((4, 19, 48, 128), f32),
            pltpu.VMEM((12, PACKET_ROWS, 128), f32),
            pltpu.VMEM((2, 19, 32, 128), f32),
            pltpu.VMEM((2, PACKET_ROWS, 128), f32),
            pltpu.VMEM((4, 19, 32, 128), f32),
            pltpu.VMEM((4, PACKET_ROWS, 128), f32),
            pltpu.VMEM((19, 48, 128), f32),
            pltpu.VMEM((19, 32, 128), f32),
            pltpu.SemaphoreType.DMA((4,)),
            pltpu.SemaphoreType.DMA((6,)),
            pltpu.SemaphoreType.DMA((6,)),
        ],
        compiler_params=pltpu.CompilerParams(
            collective_id=0, has_side_effects=True, vmem_limit_bytes=40 * 1024 * 1024
        ),
        name="lattice_step",
    )(populations, neighbours, substeps, moves)


def solution(mesh):
    sizes = (mesh.shape["gy"], mesh.shape["gz"], mesh.size)
    return jax.shard_map(
        functools.partial(shards, sizes),
        mesh=mesh,
        in_specs=(P(AXES, None, None), P(AXES, None), P(AXES), P(AXES, None)),
        out_specs=(P(AXES, None, None), P(AXES)),
        check_vma=False,
    )
```

time: 2270 us -> 35.9 us (0.02)
  the two profiles are of different devices: /device:TPU:32 before, /device:TPU:1 now
where the time goes in v1:
time: 35.9 us; the launch traced here: 35.8 us
  Pallas kernels  30.7 us (86%)
  local copies, waits for them, and re-layouts  4.4 us (12%)
  between operations  0.69 us (2%)
    pallas_call x1, Pallas kernels, shards(): pl.pallas_call(functools.partial(kernel, sizes), out_shape=(jax.ShapeDtyp...  30.7 us
    unnamed x8, local copies, waits for them, and re-layouts  2.56 us
    pallas_call x1, local copies, waits for them, and re-layouts, shards(): pl.pallas_call(functools.partial(kernel, sizes), out_shape=(jax.ShapeDtyp...  1.84 us

profile of v1, /device:TPU:1, one launch (start us, length us, event | category | flops | bytes accessed | tf_op | source)
XLA Modules:
  0.0 35.8 jit_solution(13261477361190597287)
XLA Ops:
  0.6 0.0 copy-start.2
  0.6 0.0 copy-start.1
  0.7 0.0 copy-start
  0.7 2.0 %copy.6.pop = f32[4,19,4096]{2,1,0:T(8,128)S(1)} copy(f32[4,19,4096]{2,0,1:T(4,128)} %param.4) | data formatting | bytes 2490368 | tf_op args[0]
  2.7 0.0 copy-done.2
  2.7 0.0 copy-done.1
  2.7 0.0 copy-done
  2.7 30.7 %lattice_step.1 = (f32[4,19,4096]{2,1,0:T(8,128)S(1)}, s32[4]{0:T(128)S(1)}) custom-call(f32[4,19,4096]{2,1,0:T(8,128)S(1)} %copy.6.pop, s32[4,6]{1,0:T(4,128)S(1)} %copy-done, s32[4]{0:T(128)S(1)} %copy-done.1, s32[1,2]{1,0:T(1,128)S(1)} %copy-done.2), custom_call_target="tpu_custom_call" | custom-call | tf_op jit(solution)/shard_map/lattice_step/pallas_call | solution.py:401
  33.4 1.8 %copy.7 = f32[4,19,4096]{2,0,1:T(4,128)} copy(f32[4,19,4096]{2,1,0:T(8,128)S(1)} %get-tuple-element.2) | data formatting | bytes 2490368 | tf_op jit(solution)/shard_map/lattice_step/pallas_call | solution.py:401
  35.3 0.5 %copy.9 = s32[4]{0:T(128)} copy(s32[4]{0:T(128)S(1)} %get-tuple-element.7) | data formatting | bytes 32
Async XLA Ops:
  0.6 2.1 %copy-start.2 = (s32[1,2]{1,0:T(1,128)S(1)}, s32[1,2]{1,0:T(1,128)}, u32[]{:S(2)}) copy-start(s32[1,2]{1,0:T(1,128)} %moves.1) | copy-start | bytes 28
  0.6 2.1 %copy-start.1 = (s32[4]{0:T(128)S(1)}, s32[4]{0:T(128)}, u32[]{:S(2)}) copy-start(s32[4]{0:T(128)} %sub.1) | copy-start | bytes 52
  0.7 2.1 %copy-start = (s32[4,6]{1,0:T(4,128)S(1)}, s32[4,6]{1,0:T(4,128)}, u32[]{:S(2)}) copy-start(s32[4,6]{1,0:T(4,128)} %nbr.1) | copy-start | bytes 292

commit v2 on v1

--- a/solution.py
+++ b/solution.py
@@ -36,13 +36,9 @@
 
 
 def unpacked(raw, cube, block):
-    for group in range(3):
-        count = min(8, 19 - 8 * group)
-        for part in range(4):
-            tile = raw[block, 8 * group : 8 * group + count, 1024 * part : 1024 * (part + 1)]
-            tile = tile.reshape(count, 8, 128)
-            for k in range(count):
-                cube[block, 8 * group + k, TOP + 8 * part : TOP + 8 * part + 8, :] = tile[k]
+    for q in range(19):
+        for v in range(4):
+            cube[block, q, TOP + 8 * v : TOP + 8 * v + 8, :] = raw[q, pl.ds(32 * v + block, 8, stride=4), :]
 
 
 def pack_faces(cube, packets, block, slot):
@@ -267,7 +263,7 @@
 
 def kernel(
     sizes, pop, nbr, sub, moves, out, ids, raw, cube, packets, gone, interface_out, state, interface, post, halo,
-    load_sem, send_sem, recv_sem,
+    load_sem, send_sem, recv_sem, answer_sem, near_sem, across_sem,
 ):
     ny, nz, total = sizes
     bit = ny * nz
@@ -281,24 +277,56 @@
     later = place(lax.rem(me + 1, total))
     before = place(lax.rem(me + total - 1, total))
 
+    odd = lax.rem(me // bit, 2) == 1
+    inner = lax.rem(me, bit)
+    at_start, at_end = inner == 0, inner == bit - 1
+    even = jnp.logical_not(odd)
     barrier = pltpu.get_barrier_semaphore()
-    for other in (partner, before, later):
-        pl.semaphore_signal(barrier, inc=1, device_id=other, device_id_type=MESH)
-
-    loads = [pltpu.make_async_copy(pop.at[b], raw.at[b], load_sem.at[b]) for b in range(4)]
-    for load in loads:
-        load.start()
-    for load in loads:
-        load.wait()
+
+    def signal(semaphore, device):
+        pl.semaphore_signal(semaphore, inc=1, device_id=device, device_id_type=MESH)
+
+    @pl.when(odd)
+    def _():
+        signal(barrier, partner)
+
+    @pl.when(even & at_start)
+    def _():
+        signal(barrier, before)
+
+    @pl.when(even & at_end)
+    def _():
+        signal(barrier, later)
+
+    load = pltpu.make_async_copy(pop, raw, load_sem)
+    load.start()
+    load.wait()
+
+    for b in range(4):
+        unpacked(raw, cube, b)
 
     def prepare(b, carry):
-        unpacked(raw, cube, b)
         pack_faces(cube, packets, b, b + 4)
         return carry
 
     lax.fori_loop(0, 4, prepare, 0)
 
-    pl.semaphore_wait(barrier, 3)
+    @pl.when(even)
+    def _():
+        pl.semaphore_wait(barrier, 1)
+        signal(answer_sem, partner)
+
+    @pl.when(odd)
+    def _():
+        pl.semaphore_wait(answer_sem, 1)
+
+    @pl.when(odd & jnp.logical_not(at_start))
+    def _():
+        signal(barrier, before)
+
+    @pl.when(odd & jnp.logical_not(at_end))
+    def _():
+        signal(barrier, later)
 
     def remote(source, target, number, device):
         return pltpu.make_async_remote_copy(
@@ -310,12 +338,6 @@
             device_id_type=MESH,
         )
 
-    mine = packets.at[pl.ds(4, 4), pl.ds(0, SENT_ROWS)]
-    to_later = remote(mine, packets.at[pl.ds(0, 4), pl.ds(0, SENT_ROWS)], 0, later)
-    to_before = remote(mine, packets.at[pl.ds(8, 4), pl.ds(0, SENT_ROWS)], 1, before)
-    to_later.start()
-    to_before.start()
-
     moved = [moves[0, 0], moves[0, 1]]
     blocks = []
     for k in range(2):
@@ -327,6 +349,33 @@
         copy = remote(gone.at[k], state.at[2 + k], 2 + k, partner)
         copy.start()
         blocks.append(copy)
+
+    @pl.when(odd)
+    def _():
+        pl.semaphore_wait(barrier, 2)
+        signal(near_sem, partner)
+
+    @pl.when(odd & at_start)
+    def _():
+        signal(across_sem, before)
+
+    @pl.when(odd & at_end)
+    def _():
+        signal(across_sem, later)
+
+    @pl.when(even)
+    def _():
+        pl.semaphore_wait(near_sem, 1)
+
+    @pl.when(even & (at_start | at_end))
+    def _():
+        pl.semaphore_wait(across_sem, 1)
+
+    mine = packets.at[pl.ds(4, 4), pl.ds(0, SENT_ROWS)]
+    to_later = remote(mine, packets.at[pl.ds(0, 4), pl.ds(0, SENT_ROWS)], 0, later)
+    to_before = remote(mine, packets.at[pl.ds(8, 4), pl.ds(0, SENT_ROWS)], 1, before)
+    to_later.start()
+    to_before.start()
 
     to_later.wait_recv()
     to_before.wait_recv()
@@ -377,11 +426,9 @@
         source = jnp.where(
             moved[0] == s, 2, jnp.where(moved[1] == s, 3, jnp.where(stay0 == s, 0, 1))
         )
-        for group in range(3):
-            count = min(8, 19 - 8 * group)
-            for part in range(4):
-                tile = state[source, 8 * group : 8 * group + count, 8 * part : 8 * part + 8, :]
-                out[s, 8 * group : 8 * group + count, 1024 * part : 1024 * (part + 1)] = tile.reshape(count, 1024)
+        for q in range(19):
+            for v in range(4):
+                out[q, pl.ds(32 * v + s, 8, stride=4), :] = state[source, q, 8 * v : 8 * v + 8, :]
 
     marks = [
         jnp.max(interface[2 + k, SLOT_ROW : SLOT_ROW + 1, :]).astype(jnp.int32) + partner_id * 4 for k in range(2)
@@ -398,9 +445,10 @@
 
 def shards(sizes, populations, neighbours, substeps, moves):
     f32 = jnp.float32
-    return pl.pallas_call(
+    lying = populations.reshape(4, 19, 32, 128).transpose(1, 2, 0, 3).reshape(19, 128, 128)
+    result, ids = pl.pallas_call(
         functools.partial(kernel, sizes),
-        out_shape=(jax.ShapeDtypeStruct((4, 19, 4096), f32), jax.ShapeDtypeStruct((4,), jnp.int32)),
+        out_shape=(jax.ShapeDtypeStruct((19, 128, 128), f32), jax.ShapeDtypeStruct((4,), jnp.int32)),
         in_specs=[
             pl.BlockSpec(memory_space=pl.ANY),
             pl.BlockSpec(memory_space=pltpu.SMEM),
@@ -409,7 +457,7 @@
         ],
         out_specs=(pl.BlockSpec(memory_space=pltpu.VMEM), pl.BlockSpec(memory_space=pltpu.SMEM)),
         scratch_shapes=[
-            pltpu.VMEM((4, 19, 4096), f32),
+            pltpu.VMEM((19, 128, 128), f32),
             pltpu.VMEM((4, 19, 48, 128), f32),
             pltpu.VMEM((12, PACKET_ROWS, 128), f32),
             pltpu.VMEM((2, 19, 32, 128), f32),
@@ -418,15 +466,19 @@
             pltpu.VMEM((4, PACKET_ROWS, 128), f32),
             pltpu.VMEM((19, 48, 128), f32),
             pltpu.VMEM((19, 32, 128), f32),
-            pltpu.SemaphoreType.DMA((4,)),
+            pltpu.SemaphoreType.DMA,
             pltpu.SemaphoreType.DMA((6,)),
             pltpu.SemaphoreType.DMA((6,)),
+            pltpu.SemaphoreType.REGULAR,
+            pltpu.SemaphoreType.REGULAR,
+            pltpu.SemaphoreType.REGULAR,
         ],
         compiler_params=pltpu.CompilerParams(
             collective_id=0, has_side_effects=True, vmem_limit_bytes=40 * 1024 * 1024
         ),
         name="lattice_step",
-    )(populations, neighbours, substeps, moves)
+    )(lying, neighbours, substeps, moves)
+    return result.reshape(19, 32, 4, 128).transpose(2, 0, 1, 3).reshape(4, 19, 4096), ids
 
 
 def solution(mesh):

time: 35.9 us -> 33.9 us (0.944)
  the two profiles are of different devices: /device:TPU:1 before, /device:TPU:32 now
where the time goes in v2:
time: 33.9 us; the launch traced here: 33.8 us
  Pallas kernels  28.3 us (83%)
  local copies, waits for them, and re-layouts  4.83 us (14%)
  between operations  0.65 us (2%)
    pallas_call x1, Pallas kernels, shards(): pl.pallas_call(functools.partial(kernel, sizes), out_shape=(jax.ShapeDtyp...  28.3 us
    unnamed x10, local copies, waits for them, and re-layouts  4.83 us

profile of v2, /device:TPU:32, one launch (start us, length us, event | category | flops | bytes accessed | tf_op | source)
XLA Modules:
  0.0 33.8 jit_solution(11534242320822145047)
XLA Ops:
  0.6 0.0 copy-start
  0.6 1.3 %copy-done = f32[4,19,4096]{2,0,1:T(4,128)S(1)} copy-done((f32[4,19,4096]{2,0,1:T(4,128)S(1)}, f32[4,19,4096]{2,0,1:T(4,128)}, u32[]{:S(2)}) %copy-start) | copy-done | bytes 1245208
  1.9 0.0 copy-start.1
  1.9 0.7 %copy-done.1 = s32[4,6]{1,0:T(4,128)S(1)} copy-done((s32[4,6]{1,0:T(4,128)S(1)}, s32[4,6]{1,0:T(4,128)}, u32[]{:S(2)}) %copy-start.1) | copy-done | bytes 120
  2.6 0.0 copy-start.2
  2.6 0.7 %copy-done.2 = s32[4]{0:T(128)S(1)} copy-done((s32[4]{0:T(128)S(1)}, s32[4]{0:T(128)}, u32[]{:S(2)}) %copy-start.2) | copy-done | bytes 40
  3.3 0.0 copy-start.3
  3.3 0.7 %copy-done.3 = s32[1,2]{1,0:T(1,128)S(1)} copy-done((s32[1,2]{1,0:T(1,128)S(1)}, s32[1,2]{1,0:T(1,128)}, u32[]{:S(2)}) %copy-start.3) | copy-done | bytes 32
  3.9 28.3 %lattice_step.1 = (f32[19,128,128]{2,1,0:T(8,128)S(1)}, s32[4]{0:T(128)S(1)}) custom-call(f32[19,128,128]{2,1,0:T(8,128)S(1)} %bitcast.11, s32[4,6]{1,0:T(4,128)S(1)} %copy-done.1, s32[4]{0:T(128)S(1)} %copy-done.2, s32[1,2]{1,0:T(1,128)S(1)} %copy-done.3), custom_call_target="tpu_custom_call" | custom-call | tf_op jit(solution)/shard_map/lattice_step/pallas_call | solution.py:449
  32.2 1.0 %copy.10 = f32[4,19,4096]{2,0,1:T(4,128)} copy(f32[4,19,4096]{2,0,1:T(4,128)S(1)} %bitcast.10) | data formatting | bytes 2490368
  33.3 0.5 %copy.11 = s32[4]{0:T(128)} copy(s32[4]{0:T(128)S(1)} %get-tuple-element.9) | data formatting | bytes 32
Async XLA Ops:
  0.6 1.3 %copy-start = (f32[4,19,4096]{2,0,1:T(4,128)S(1)}, f32[4,19,4096]{2,0,1:T(4,128)}, u32[]{:S(2)}) copy-start(f32[4,19,4096]{2,0,1:T(4,128)} %param.4) | copy-start | bytes 3735556
  1.9 0.7 %copy-start.1 = (s32[4,6]{1,0:T(4,128)S(1)}, s32[4,6]{1,0:T(4,128)}, u32[]{:S(2)}) copy-start(s32[4,6]{1,0:T(4,128)} %nbr.1) | copy-start | bytes 292
  2.6 0.7 %copy-start.2 = (s32[4]{0:T(128)S(1)}, s32[4]{0:T(128)}, u32[]{:S(2)}) copy-start(s32[4]{0:T(128)} %sub.1) | copy-start | bytes 52
  3.3 0.7 %copy-start.3 = (s32[1,2]{1,0:T(1,128)S(1)}, s32[1,2]{1,0:T(1,128)}, u32[]{:S(2)}) copy-start(s32[1,2]{1,0:T(1,128)} %moves.1) | copy-start | bytes 28

commit v3 on v2

v3 whole, which is shorter than its diff:
```python
import functools

import jax
import jax.numpy as jnp
import numpy as np
from jax import lax
from jax.experimental import pallas as pl
from jax.experimental.pallas import tpu as pltpu
from jax.sharding import PartitionSpec as P

MESH = pl.DeviceIdType.MESH
AXES = ("gx", "gy", "gz")
VELOCITY = [
    (0, 0, 0), (1, 0, 0), (-1, 0, 0), (0, 1, 0), (0, -1, 0), (0, 0, 1), (0, 0, -1),
    (1, 1, 0), (-1, -1, 0), (1, -1, 0), (-1, 1, 0), (1, 0, 1), (-1, 0, -1),
    (1, 0, -1), (-1, 0, 1), (0, 1, 1), (0, -1, -1), (0, 1, -1), (0, -1, 1),
]
OPPOSITE = [0, 2, 1, 4, 3, 6, 5, 8, 7, 10, 9, 12, 11, 14, 13, 16, 15, 18, 17]
LEAVING = [
    [2, 8, 10, 12, 14], [1, 7, 9, 11, 13], [4, 8, 9, 16, 18],
    [3, 7, 10, 15, 17], [6, 12, 13, 16, 17], [5, 11, 14, 15, 18],
]
Y_SENT, Z_SENT, X_SENT, COUNT_ROW, SLOT_ROW, SENT_ROWS = 0, 24, 48, 68, 69, 72
X_ROW, Y_ROW, Z_ROW, PLANE_ROWS = 0, 24, 56, 96
TOP = 8


def turned(value, by):
    by = by % 128
    return value if by == 0 else pltpu.roll(value, by, 1)


def grid_iotas():
    row = lax.broadcasted_iota(jnp.int32, (8, 128), 0)
    lane = lax.broadcasted_iota(jnp.int32, (8, 128), 1)
    return row, lane


def unpacked(raw, cube, block):
    for q in range(19):
        for v in range(4):
            cube[block, q, TOP + 8 * v : TOP + 8 * v + 8, :] = raw[q, pl.ds(32 * v + block, 8, stride=4), :]


def pack_faces(cube, packets, block, slot):
    row, lane = grid_iotas()
    even = row % 2 == 0
    place = (lane // 16 - row % 2) % 8
    for face in range(2):
        start = TOP if face == 0 else TOP + 30
        for k in range(5):
            at = X_SENT + 10 * face + 2 * k
            packets[slot, at : at + 2, :] = cube[block, LEAVING[face][k], start : start + 2, :]
    ys, zs = [], []
    for v in range(4):
        base = TOP + 8 * v
        kept = jnp.zeros((8, 128), jnp.float32)
        for k in range(5):
            far = cube[block, LEAVING[3][k], base + 1 : base + 9, :]
            near = cube[block, LEAVING[2][k], base - 1 : base + 7, :]
            moved = turned(jnp.where(even, far, near), 16 * (k + 1))
            kept = jnp.where(place == k, moved, kept)
        ys.append(kept)
        kept = jnp.zeros((8, 128), jnp.float32)
        for k in range(5):
            near = cube[block, LEAVING[4][k], base : base + 8, :]
            far = cube[block, LEAVING[5][k], base : base + 8, :]
            moved = turned(jnp.where(lane % 16 == 15, far, near), 2 * k + 1)
            kept = jnp.where(lane % 16 // 2 == k, moved, kept)
        zs.append(kept)
    ys[0] = jnp.where(place >= 5, turned(ys[3], 80), ys[0])
    ys[1] = jnp.where(place >= 5, turned(ys[3], 32), ys[1])
    zs[0] = jnp.where(lane % 16 >= 10, turned(zs[3], 10), zs[0])
    zs[1] = jnp.where(lane % 16 >= 10, turned(zs[3], 4), zs[1])
    for v in range(3):
        packets[slot, Y_SENT + 8 * v : Y_SENT + 8 * v + 8, :] = ys[v]
        packets[slot, Z_SENT + 8 * v : Z_SENT + 8 * v + 8, :] = zs[v]


def spread(sent, slot, planes):
    row, lane = grid_iotas()
    place = (lane // 16 - row % 2) % 8
    ys = [sent[slot, Y_SENT + 8 * v : Y_SENT + 8 * v + 8, :] for v in range(3)]
    zs = [sent[slot, Z_SENT + 8 * v : Z_SENT + 8 * v + 8, :] for v in range(3)]
    ys.append(jnp.where(place < 3, turned(ys[0], -80), turned(ys[1], -32)))
    zs.append(jnp.where(lane % 16 < 6, turned(zs[0], -10), turned(zs[1], -4)))
    for v in range(4):
        planes[Y_ROW + 8 * v : Y_ROW + 8 * v + 8, :] = ys[v]
        planes[Z_ROW + 8 * v : Z_ROW + 8 * v + 8, :] = zs[v]
    for v in range(3):
        planes[X_ROW + 8 * v : X_ROW + 8 * v + 8, :] = sent[slot, X_SENT + 8 * v : X_SENT + 8 * v + 8, :]


def assemble(packets, plan, block, first, out, slot, mark):
    row, lane = grid_iotas()
    at, valid = [], []
    for face in range(6):
        near = plan[block, face]
        valid.append(jnp.full((8, 128), near, jnp.int32) >= 0)
        at.append(jnp.clip(near - first, 0, 11))
    for face in range(2):
        other = 10 * (face ^ 1)
        for start, rows in ((0, 8), (8, 2)):
            value = packets[at[face], X_SENT + other + start : X_SENT + other + start + rows, :]
            out[slot, X_SENT + 10 * face + start : X_SENT + 10 * face + start + rows, :] = jnp.where(
                valid[face][:rows], value, -1.0
            )
    for v in range(3):
        rows = slice(Y_SENT + 8 * v, Y_SENT + 8 * v + 8)
        even_rows = jnp.where(valid[2], packets[at[2], rows, :], -1.0)
        odd_rows = jnp.where(valid[3], packets[at[3], rows, :], -1.0)
        out[slot, rows, :] = jnp.where(row % 2 == 0, even_rows, odd_rows)
        rows = slice(Z_SENT + 8 * v, Z_SENT + 8 * v + 8)
        low = jnp.where(valid[4], packets[at[4], rows, :], -1.0)
        high = jnp.where(valid[5], packets[at[5], rows, :], -1.0)
        out[slot, rows, :] = jnp.where(lane % 2 == 0, low, high)
    count = jnp.full((1, 128), plan[4, block], jnp.int32).astype(jnp.float32)
    out[slot, COUNT_ROW : COUNT_ROW + 1, :] = count
    out[slot, SLOT_ROW : SLOT_ROW + 1, :] = jnp.full((1, 128), mark, jnp.int32).astype(jnp.float32)


def outside(which, v):
    row, lane = grid_iotas()
    cx, cy, cz = VELOCITY[which]
    x_mask = y_mask = z_mask = None
    if cx == 1 and v == 0:
        x_mask = row < 2
    if cx == -1 and v == 3:
        x_mask = row >= 6
    if cy == 1:
        y_mask = (row % 2 == 0) & (lane < 16)
    if cy == -1:
        y_mask = (row % 2 == 1) & (lane >= 112)
    if cz == 1:
        z_mask = lane % 16 == 0
    if cz == -1:
        z_mask = lane % 16 == 15
    return x_mask, y_mask, z_mask


def build_halo(planes, halo):
    row, lane = grid_iotas()
    for which in range(1, 19):
        cx, cy, cz = VELOCITY[which]
        for v in range(4):
            x_mask, y_mask, z_mask = outside(which, v)
            value = None
            if z_mask is not None:
                face = 4 if cz == 1 else 5
                k = LEAVING[face ^ 1].index(which)
                by = 16 * cy - (2 * k + 1) + (-15 if cz == 1 else 15)
                start = Z_ROW + 8 * v - 2 * cx
                value = turned(planes[start : start + 8, :], by)
                if cy != 0:
                    start = start - cy
                    beside = turned(planes[start : start + 8, :], by)
                    value = jnp.where(lane < 16 if cy == 1 else lane >= 112, beside, value)
            if y_mask is not None:
                face = 2 if cy == 1 else 3
                k = LEAVING[face ^ 1].index(which)
                by = -16 * k if cy == 1 else 112 - 16 * (k + 1)
                start = Y_ROW + 8 * v - 2 * cx
                plane = planes[start : start + 8, :]
                line = turned(plane, by)
                if cz != 0:
                    line = jnp.where(lane % 16 == (0 if cz == 1 else 15), line, turned(plane, by + cz))
                value = line if value is None else jnp.where(y_mask, line, value)
            if x_mask is not None:
                face = 0 if cx == 1 else 1
                k = LEAVING[face ^ 1].index(which)
                at = X_ROW + 10 * face + 2 * k
                pair = planes[at : at + 2, :]
                upper, lower = pair[0:1], pair[1:2]
                if cy == 1:
                    high, low = turned(upper, 16), turned(lower, 16)
                    lane1 = lane[0:1]
                    lower = jnp.where(lane1 < 16, high, low)
                    upper = jnp.where(lane1 < 16, upper, high)
                elif cy == -1:
                    high, low = turned(upper, -16), turned(lower, -16)
                    lane1 = lane[0:1]
                    upper = jnp.where(lane1 >= 112, low, high)
                    lower = jnp.where(lane1 >= 112, lower, low)
                elif cz != 0:
                    edge = lane[0:1] % 16 == (0 if cz == 1 else 15)
                    upper = jnp.where(edge, upper, turned(upper, cz))
                    lower = jnp.where(edge, lower, turned(lower, cz))
                both = jnp.where(
                    row % 2 == 0,
                    jnp.broadcast_to(upper, (8, 128)),
                    jnp.broadcast_to(lower, (8, 128)),
                )
                value = both if value is None else jnp.where(x_mask, both, value)
            if value is not None:
                halo[which, 8 * v : 8 * v + 8, :] = value


def collide(f, shear):
    s = {q: f[q] + f[q + 1] for q in range(1, 19, 2)}
    d = {q: f[q] - f[q + 1] for q in range(1, 19, 2)}
    sx, sy, sz = s[1], s[3], s[5]
    sxy, sxz, syz = s[7] + s[9], s[11] + s[13], s[15] + s[17]
    along = sx + (sy + sz)
    across = sxy + (sxz + syz)
    xa, xb = d[7] + d[9], d[11] + d[13]
    ya, yb = d[15] + d[17], d[7] - d[9]
    za, zb = d[11] - d[13], d[15] - d[17]
    x_sum, y_sum, z_sum = xa + xb, ya + yb, za + zb
    jx, jy, jz = d[1] + x_sum, d[3] + y_sum, d[5] + z_sum
    xx, yy, zz = jx * jx, jy * jy, jz * jz
    yz_sum = yy + zz
    jj = xx + yz_sum
    e1 = (1.19 * 19.0 / 2394.0) * ((across - f[0]) - jj)
    e2 = (1.4 / 252.0) * ((9.0 * f[0] - 7.0 * along) - (2.0 * across - 5.5 * jj))
    qx = (1.2 / 40.0 * 5.0 / 3.0) * (x_sum - 2.0 * d[1])
    qy = (1.2 / 40.0 * 5.0 / 3.0) * (y_sum - 2.0 * d[3])
    qz = (1.2 / 40.0 * 5.0 / 3.0) * (z_sum - 2.0 * d[5])
    axial = (2.0 * sx) - (sy + sz)
    planar = (sxy + sxz) - 2.0 * syz
    stress = 2.0 * xx - yz_sum
    e9 = (shear * (1.0 / 36.0)) * ((axial + planar) - stress)
    e10 = (1.4 / 72.0) * ((planar - 2.0 * axial) + 0.5 * stress)
    axial_w = sy - sz
    planar_w = sxy - sxz
    stress_w = yy - zz
    e11 = (shear * (1.0 / 12.0)) * ((axial_w + planar_w) - stress_w)
    e12 = (1.4 / 24.0) * ((planar_w - 2.0 * axial_w) + 0.5 * stress_w)
    quarter = shear * 0.25
    e13 = quarter * ((s[7] - s[9]) - jx * jy)
    e14 = quarter * ((s[15] - s[17]) - jy * jz)
    e15 = quarter * ((s[11] - s[13]) - jx * jz)
    e16 = (1.98 / 8.0) * (xa - xb)
    e17 = (1.98 / 8.0) * (ya - yb)
    e18 = (1.98 / 8.0) * (za - zb)
    post = [None] * 19
    post[0] = f[0] + (30.0 * e1 - 12.0 * e2)
    base = 11.0 * e1 + 4.0 * e2
    t9 = e9 - 2.0 * e10
    t11 = e11 - 2.0 * e12
    evens = {1: 2.0 * t9 - base, 3: t11 - (t9 + base), 5: -((t11 + t9) + base)}
    base = 8.0 * e1 + e2
    u9 = e9 + e10
    u11 = e11 + e12
    upper, lower, third = base + u9 + u11, base + u9 - u11, base - 2.0 * u9
    evens.update({7: upper + e13, 9: upper - e13, 11: lower + e15, 13: lower - e15, 15: third + e14, 17: third - e14})
    xp, xm = qx + e16, qx - e16
    yp, ym = qy + e17, qy - e17
    zp, zm = qz + e18, qz - e18
    odds = {
        1: -4.0 * qx, 3: -4.0 * qy, 5: -4.0 * qz,
        7: xp + ym, 9: xp - ym, 11: xm + zp, 13: xm - zp, 15: yp + zm, 17: yp - zm,
    }
    for q in range(1, 19, 2):
        post[q] = f[q] - (evens[q] + odds[q])
        post[q + 1] = f[q + 1] - (evens[q] - odds[q])
    return post


def arrived(q, v, post, halo):
    _, lane = grid_iotas()
    cx, cy, cz = VELOCITY[q]
    start = TOP + 8 * v - 2 * cx
    value = post[q, start : start + 8, :]
    by = 16 * cy + cz
    if cy != 0:
        beside = post[q, start - cy : start - cy + 8, :]
        value = jnp.where(lane >= 128 - by if cy == 1 else lane < -by, beside, value)
    value = turned(value, by)
    masks = [m for m in outside(q, v) if m is not None]
    if masks:
        edge = halo[q, 8 * v : 8 * v + 8, :]
        bounced = post[OPPOSITE[q], TOP + 8 * v : TOP + 8 * v + 8, :]
        value = jnp.where(functools.reduce(jnp.logical_or, masks), jnp.where(edge < 0.0, bounced, edge), value)
    return value


def collide_first(first, post, shear):
    for v in range(4):
        values = collide([first[q, 8 * v : 8 * v + 8, :] for q in range(19)], shear)
        for q in range(19):
            post[q, TOP + 8 * v : TOP + 8 * v + 8, :] = values[q]


def run_and_collide(state, post, target, halo, shear):
    for v in range(4):
        values = [arrived(q, v, post, halo) for q in range(19)]
        for q in range(19):
            state[q, 8 * v : 8 * v + 8, :] = values[q]
        values = collide(values, shear)
        for q in range(19):
            target[q, TOP + 8 * v : TOP + 8 * v + 8, :] = values[q]


def run_last(state, post, halo):
    for v in range(4):
        for q in range(19):
            state[q, 8 * v : 8 * v + 8, :] = arrived(q, v, post, halo)


def kernel(
    sizes, pop, plan_in, out, ids, raw, plan, theirs, state, cube, packets, gone, interface_out, first, interface, planes, post, halo,
    load_sem, send_sem, recv_sem, answer_sem, near_sem, across_sem,
):
    ny, nz, total = sizes
    bit = ny * nz
    me = lax.axis_index("gx") * bit + lax.axis_index("gy") * nz + lax.axis_index("gz")

    def place(d):
        return (d // bit, d // nz % ny, d % nz)

    partner_id = lax.rem(me // bit, 2) * (-2 * bit) + bit + me
    partner = place(partner_id)
    later = place(lax.rem(me + 1, total))
    before = place(lax.rem(me + total - 1, total))

    loads = [
        pltpu.make_async_copy(source, target, load_sem.at[k]) for k, (source, target) in enumerate(((plan_in, plan), (pop, raw)))
    ]
    for load in loads:
        load.start()

    odd = lax.rem(me // bit, 2) == 1
    inner = lax.rem(me, bit)
    at_start, at_end = inner == 0, inner == bit - 1
    even = jnp.logical_not(odd)
    barrier = pltpu.get_barrier_semaphore()

    def signal(semaphore, device):
        pl.semaphore_signal(semaphore, inc=1, device_id=device, device_id_type=MESH)

    @pl.when(odd)
    def _():
        signal(barrier, partner)

    @pl.when(even & at_start)
    def _():
        signal(barrier, before)

    @pl.when(even & at_end)
    def _():
        signal(barrier, later)

    def remote(source, target, number, device):
        return pltpu.make_async_remote_copy(
            src_ref=source,
            dst_ref=target,
            send_sem=send_sem.at[number],
            recv_sem=recv_sem.at[number],
            device_id=device,
            device_id_type=MESH,
        )

    @pl.when(even)
    def _():
        pl.semaphore_wait(barrier, 1)
        signal(answer_sem, partner)

    @pl.when(odd)
    def _():
        pl.semaphore_wait(answer_sem, 1)

    @pl.when(odd & jnp.logical_not(at_start))
    def _():
        signal(barrier, before)

    @pl.when(odd & jnp.logical_not(at_end))
    def _():
        signal(barrier, later)

    for load in loads:
        load.wait()

    moved = [plan[5, 0], plan[5, 1]]
    for k in range(2):
        for q in range(19):
            for v in range(4):
                gone[k, q, 8 * v : 8 * v + 8, :] = raw[q, pl.ds(32 * v + moved[k], 8, stride=4), :]

    orders = remote(plan, theirs, 12, partner)
    orders.start()
    blocks = [remote(gone.at[k], first.at[2 + k], k, partner) for k in range(2)]
    for copy in blocks:
        copy.start()

    @pl.when(odd)
    def _():
        pl.semaphore_wait(barrier, 2)
        signal(near_sem, partner)

    @pl.when(odd & at_start)
    def _():
        signal(across_sem, before)

    @pl.when(odd & at_end)
    def _():
        signal(across_sem, later)

    for b in range(4):
        unpacked(raw, cube, b)

    pack_faces(cube, packets, 0, 4)

    @pl.when(even)
    def _():
        pl.semaphore_wait(near_sem, 1)

    @pl.when(even & (at_start | at_end))
    def _():
        pl.semaphore_wait(across_sem, 1)

    halos = []
    for b in range(4):
        if b > 0:
            pack_faces(cube, packets, b, 4 + b)
        for number, at, device in ((4 + b, b, later), (8 + b, 8 + b, before)):
            copy = remote(packets.at[4 + b], packets.at[at], number, device)
            copy.start()
            halos.append(copy)
    low = jnp.minimum(moved[0], moved[1])
    high = jnp.maximum(moved[0], moved[1])
    stay0 = jnp.where(low > 0, 0, jnp.where(high > 1, 1, 2))
    stay1 = jnp.minimum(6 - low - high - stay0, 3)

    def keep(j, carry):
        stay = jnp.where(j == 0, stay0, stay1)

        def one(q, inner_carry):
            first[j, q] = cube[stay, q, TOP : TOP + 32, :]
            return inner_carry

        lax.fori_loop(0, 19, one, 0)
        count = jnp.full((8, 128), plan[4, stay], jnp.int32).astype(jnp.float32)
        collide_first(first.at[j], post.at[j, 0], 1.0 / (count * (1.0 / 1.6 - 0.5) + 0.5))
        return carry

    lax.fori_loop(0, 2, keep, 0)

    for copy in halos:
        copy.wait_recv()

    lowest = (me - 1) * 4
    faces = []
    for k in range(2):
        assemble(packets, plan, moved[k], lowest, interface_out, k, moved[k])
        copy = remote(interface_out.at[k], interface.at[2 + k], 2 + k, partner)
        copy.start()
        faces.append(copy)

    for j, stay in enumerate((stay0, stay1)):
        assemble(packets, plan, stay, lowest, interface, j, stay)

    def job(j, carry):
        for k in range(2):
            @pl.when(j == 2 + k)
            def _(k=k):
                faces[k].wait_recv()
                blocks[k].wait_recv()

        count = jnp.broadcast_to(interface[j, COUNT_ROW : COUNT_ROW + 1, :], (8, 128))
        shear = 1.0 / (count * (1.0 / 1.6 - 0.5) + 0.5)
        spread(interface, j, planes)
        build_halo(planes, halo)

        @pl.when(j >= 2)
        def _():
            collide_first(first.at[j], post.at[j, 0], shear)

        def one(step, inner_carry):
            now = lax.rem(step, 2)
            run_and_collide(state.at[step, j], post.at[j, now], post.at[j, 1 - now], halo, shear)
            return inner_carry

        lax.fori_loop(0, 3, one, 0)
        run_last(state.at[3, j], post.at[j, 1], halo)
        return carry

    lax.fori_loop(0, 4, job, 0)

    orders.wait_recv()
    for s in range(4):
        here = jnp.where(moved[0] == s, 2, jnp.where(moved[1] == s, 3, jnp.where(stay0 == s, 0, 1)))
        sent = jnp.where(moved[0] == s, theirs[5, 0], theirs[5, 1])
        foreign = here >= 2
        count = jnp.where(foreign, theirs[4, jnp.clip(sent, 0, 3)], plan[4, s])
        step = jnp.clip(count - 1, 0, 3)
        for q in range(19):
            for v in range(4):
                out[q, pl.ds(32 * v + s, 8, stride=4), :] = state[step, here, q, 8 * v : 8 * v + 8, :]
        ids[s] = jnp.where(foreign, partner_id * 4 + sent, me * 4 + s)

    for copy in halos + blocks + faces + [orders]:
        copy.wait_send()


def write(result, ids_in, out, ids, sems):
    copies = [pltpu.make_async_copy(result, out, sems.at[0]), pltpu.make_async_copy(ids_in, ids, sems.at[1])]
    for copy in copies:
        copy.start()
    for copy in copies:
        copy.wait()


def shards(sizes, populations, neighbours, substeps, moves):
    f32 = jnp.float32
    lying = populations.reshape(4, 19, 32, 128).transpose(1, 2, 0, 3).reshape(19, 128, 128)
    plan = jnp.concatenate(
        [neighbours, jnp.pad(substeps[None], ((0, 0), (0, 2))), jnp.pad(moves, ((0, 0), (0, 4)))], axis=0
    )
    vmem, smem = pl.BlockSpec(memory_space=pltpu.VMEM), pl.BlockSpec(memory_space=pltpu.SMEM)
    whole = pl.BlockSpec(memory_space=pl.ANY)
    shapes = (jax.ShapeDtypeStruct((19, 128, 128), f32), jax.ShapeDtypeStruct((4,), jnp.int32))
    result, ids = pl.pallas_call(
        functools.partial(kernel, sizes),
        out_shape=shapes,
        in_specs=[whole, whole],
        out_specs=(vmem, smem),
        scratch_shapes=[
            pltpu.VMEM((19, 128, 128), f32),
            pltpu.SMEM((6, 6), jnp.int32),
            pltpu.SMEM((6, 6), jnp.int32),
            pltpu.VMEM((4, 4, 19, 32, 128), f32),
            pltpu.VMEM((4, 19, 48, 128), f32),
            pltpu.VMEM((12, SENT_ROWS, 128), f32),
            pltpu.VMEM((2, 19, 32, 128), f32),
            pltpu.VMEM((2, SENT_ROWS, 128), f32),
            pltpu.VMEM((4, 19, 32, 128), f32),
            pltpu.VMEM((4, SENT_ROWS, 128), f32),
            pltpu.VMEM((PLANE_ROWS, 128), f32),
            pltpu.VMEM((4, 2, 19, 48, 128), f32),
            pltpu.VMEM((19, 32, 128), f32),
            pltpu.SemaphoreType.DMA((2,)),
            pltpu.SemaphoreType.DMA((13,)),
            pltpu.SemaphoreType.DMA((13,)),
            pltpu.SemaphoreType.REGULAR,
            pltpu.SemaphoreType.REGULAR,
            pltpu.SemaphoreType.REGULAR,
        ],
        compiler_params=pltpu.CompilerParams(
            collective_id=0, has_side_effects=True, vmem_limit_bytes=53500 * 1024
        ),
        name="lattice_step",
    )(lying, plan)
    result, ids = pl.pallas_call(
        write,
        out_shape=shapes,
        in_specs=[vmem, whole],
        out_specs=(whole, whole),
        scratch_shapes=[pltpu.SemaphoreType.DMA((2,))],
        compiler_params=pltpu.CompilerParams(vmem_limit_bytes=36 * 1024 * 1024),
        name="write_out",
    )(result, ids)
    return result.reshape(19, 32, 4, 128).transpose(2, 0, 1, 3).reshape(4, 19, 4096), ids


def solution(mesh):
    sizes = (mesh.shape["gy"], mesh.shape["gz"], mesh.size)
    return jax.shard_map(
        functools.partial(shards, sizes),
        mesh=mesh,
        in_specs=(P(AXES, None, None), P(AXES, None), P(AXES), P(AXES, None)),
        out_specs=(P(AXES, None, None), P(AXES)),
        check_vma=False,
    )
```

time: 33.9 us -> 30.7 us (0.906)
  local copies, waits for them, and re-layouts: 4.83 us -> 0 us
  Pallas kernels: 28.3 us -> 29.2 us
  other arithmetic: 0 us -> 0.72 us
    unnamed x10 -> x0, local copies, waits for them, and re-layouts: 4.83 us -> none
    pallas_call x1 -> x2, Pallas kernels: 28.3 us -> 29.2 us  [the longest x1 28.1 us: shards(): pl.pallas_call(functools.partial(kernel, sizes), out_shape=shapes, in_spe...]
    concatenate x0 -> x1, other arithmetic: none -> 0.72 us  [shards(): jnp.concatenate([neighbours, jnp.pad(substeps[None], ((0, 0), (0, 2))), j...]
where the time goes in v3:
time: 30.7 us; the launch traced here: 30.6 us
  Pallas kernels  29.2 us (95%)
  other arithmetic  0.72 us (2%)
  between operations  0.64 us (2%)
    pallas_call x1, Pallas kernels, shards(): pl.pallas_call(functools.partial(kernel, sizes), out_shape=shapes, in_spe...  28.1 us
    pallas_call x1, Pallas kernels, shards(): pl.pallas_call(write, out_shape=shapes, in_specs=[vmem, whole], out_specs...  1.06 us
    concatenate x1, other arithmetic, shards(): jnp.concatenate([neighbours, jnp.pad(substeps[None], ((0, 0), (0, 2))), j...  0.72 us

profile of v3, /device:TPU:32, one launch (start us, length us, event | category | flops | bytes accessed | tf_op | source)
XLA Modules:
  0.0 30.6 jit_solution(18214945787293083297)
XLA Ops:
  0.6 0.7 %pad_add_fusion.plan_in = s32[6,6]{1,0:T(8,128)S(1)} fusion(s32[1,2]{1,0:T(1,128)} %param.7, s32[1,4]{1,0:T(1,128)} %bitcast.12, s32[4,6]{1,0:T(4,128)} %param.5), kind=kLoop, calls=%fused_computation | loop fusion | flops 72 | bytes 264 | tf_op jit(solution)/shard_map/concatenate | solution.py:506
  1.4 28.1 %lattice_step.1 = (f32[19,128,128]{2,1,0:T(8,128)S(1)}, s32[4]{0:T(128)S(1)}) custom-call(f32[19,128,128]{2,1,0:T(8,128)} %bitcast.11, s32[6,6]{1,0:T(8,128)S(1)} %pad_add_fusion.plan_in), custom_call_target="tpu_custom_call" | custom-call | tf_op jit(solution)/shard_map/lattice_step/pallas_call | solution.py:512
  29.5 1.1 %write_out.1 = (f32[19,128,128]{2,1,0:T(8,128)}, s32[4]{0:T(128)}) custom-call(f32[19,128,128]{2,1,0:T(8,128)S(1)} %get-tuple-element.6.result, s32[4]{0:T(128)S(1)} %get-tuple-element.7.ids_in), custom_call_target="tpu_custom_call" | custom-call | tf_op jit(solution)/shard_map/write_out/pallas_call | solution.py:543

commit v4 on v3

--- a/solution.py
+++ b/solution.py
@@ -20,7 +20,7 @@
     [2, 8, 10, 12, 14], [1, 7, 9, 11, 13], [4, 8, 9, 16, 18],
     [3, 7, 10, 15, 17], [6, 12, 13, 16, 17], [5, 11, 14, 15, 18],
 ]
-Y_SENT, Z_SENT, X_SENT, COUNT_ROW, SLOT_ROW, SENT_ROWS = 0, 24, 48, 68, 69, 72
+Y_SENT, Z_SENT, X_SENT, SENT_ROWS = 0, 24, 48, 64
 X_ROW, Y_ROW, Z_ROW, PLANE_ROWS = 0, 24, 56, 96
 TOP = 8
 
@@ -42,15 +42,20 @@
             cube[block, q, TOP + 8 * v : TOP + 8 * v + 8, :] = raw[q, pl.ds(32 * v + block, 8, stride=4), :]
 
 
-def pack_faces(cube, packets, block, slot):
+def pack_faces(cube, packets, block, slot, corner):
     row, lane = grid_iotas()
     even = row % 2 == 0
     place = (lane // 16 - row % 2) % 8
     for face in range(2):
         start = TOP if face == 0 else TOP + 30
         for k in range(5):
-            at = X_SENT + 10 * face + 2 * k
-            packets[slot, at : at + 2, :] = cube[block, LEAVING[face][k], start : start + 2, :]
+            at = 10 * face + 2 * k
+            pair = cube[block, LEAVING[face][k], start : start + 2, :]
+            if at < 16:
+                packets[slot, X_SENT + at : X_SENT + at + 2, :] = pair
+            else:
+                corner[at - 16 : at - 14, :] = pair
+                corner[at - 12 : at - 10, :] = pair
     ys, zs = [], []
     for v in range(4):
         base = TOP + 8 * v
@@ -72,6 +77,10 @@
     ys[1] = jnp.where(place >= 5, turned(ys[3], 32), ys[1])
     zs[0] = jnp.where(lane % 16 >= 10, turned(zs[3], 10), zs[0])
     zs[1] = jnp.where(lane % 16 >= 10, turned(zs[3], 4), zs[1])
+    rest = corner[...]
+    rest = jnp.where(row < 4, rest, turned(rest, 64))
+    ys[1] = jnp.where(place == 7, jnp.where(even, turned(rest, 64), turned(rest, 80)), ys[1])
+    ys[2] = jnp.where(place >= 5, jnp.where(even, turned(rest, 80), turned(rest, 96)), ys[2])
     for v in range(3):
         packets[slot, Y_SENT + 8 * v : Y_SENT + 8 * v + 8, :] = ys[v]
         packets[slot, Z_SENT + 8 * v : Z_SENT + 8 * v + 8, :] = zs[v]
@@ -87,36 +96,40 @@
     for v in range(4):
         planes[Y_ROW + 8 * v : Y_ROW + 8 * v + 8, :] = ys[v]
         planes[Z_ROW + 8 * v : Z_ROW + 8 * v + 8, :] = zs[v]
-    for v in range(3):
+    for v in range(2):
         planes[X_ROW + 8 * v : X_ROW + 8 * v + 8, :] = sent[slot, X_SENT + 8 * v : X_SENT + 8 * v + 8, :]
-
-
-def assemble(packets, plan, block, first, out, slot, mark):
+    even = row % 2 == 0
+    one = jnp.where(even, turned(ys[1], -64), turned(ys[1], -80))
+    rest = jnp.where(lane // 16 == 3, one, jnp.where(even, turned(ys[2], -80), turned(ys[2], -96)))
+    planes[X_ROW + 16 : X_ROW + 24, :] = rest
+    below = turned(planes[X_ROW + 20 : X_ROW + 28, :], 64)
+    planes[X_ROW + 16 : X_ROW + 20, :] = jnp.where(lane < 64, rest, below)[0:4]
+
+
+def assemble(packets, plan, block, first, out, slot):
     row, lane = grid_iotas()
     at, valid = [], []
     for face in range(6):
         near = plan[block, face]
         valid.append(jnp.full((8, 128), near, jnp.int32) >= 0)
         at.append(jnp.clip(near - first, 0, 11))
-    for face in range(2):
-        other = 10 * (face ^ 1)
-        for start, rows in ((0, 8), (8, 2)):
-            value = packets[at[face], X_SENT + other + start : X_SENT + other + start + rows, :]
-            out[slot, X_SENT + 10 * face + start : X_SENT + 10 * face + start + rows, :] = jnp.where(
-                valid[face][:rows], value, -1.0
-            )
+    place = (lane // 16 - row % 2) % 8
+    upper, lower = slice(X_SENT, X_SENT + 8), slice(X_SENT + 8, X_SENT + 16)
+    out[slot, upper, :] = jnp.where(valid[1], packets[at[1], upper, :], -1.0)
+    second = jnp.where(valid[1], packets[at[1], lower, :], -1.0)
+    out[slot, lower, :] = jnp.where(row < 2, second, jnp.where(valid[0], packets[at[0], lower, :], -1.0))
     for v in range(3):
         rows = slice(Y_SENT + 8 * v, Y_SENT + 8 * v + 8)
         even_rows = jnp.where(valid[2], packets[at[2], rows, :], -1.0)
         odd_rows = jnp.where(valid[3], packets[at[3], rows, :], -1.0)
-        out[slot, rows, :] = jnp.where(row % 2 == 0, even_rows, odd_rows)
+        value = jnp.where(row % 2 == 0, even_rows, odd_rows)
+        if v > 0:
+            value = jnp.where(place >= (7 if v == 1 else 5), jnp.where(valid[0], packets[at[0], rows, :], -1.0), value)
+        out[slot, rows, :] = value
         rows = slice(Z_SENT + 8 * v, Z_SENT + 8 * v + 8)
         low = jnp.where(valid[4], packets[at[4], rows, :], -1.0)
         high = jnp.where(valid[5], packets[at[5], rows, :], -1.0)
         out[slot, rows, :] = jnp.where(lane % 2 == 0, low, high)
-    count = jnp.full((1, 128), plan[4, block], jnp.int32).astype(jnp.float32)
-    out[slot, COUNT_ROW : COUNT_ROW + 1, :] = count
-    out[slot, SLOT_ROW : SLOT_ROW + 1, :] = jnp.full((1, 128), mark, jnp.int32).astype(jnp.float32)
 
 
 def outside(which, v):
@@ -150,11 +163,12 @@
                 k = LEAVING[face ^ 1].index(which)
                 by = 16 * cy - (2 * k + 1) + (-15 if cz == 1 else 15)
                 start = Z_ROW + 8 * v - 2 * cx
-                value = turned(planes[start : start + 8, :], by)
+                value = planes[start : start + 8, :]
                 if cy != 0:
-                    start = start - cy
-                    beside = turned(planes[start : start + 8, :], by)
-                    value = jnp.where(lane < 16 if cy == 1 else lane >= 112, beside, value)
+                    beside = planes[start - cy : start - cy + 8, :]
+                    to = (lane + by) % 128
+                    value = jnp.where(to < 16 if cy == 1 else to >= 112, beside, value)
+                value = turned(value, by)
             if y_mask is not None:
                 face = 2 if cy == 1 else 3
                 k = LEAVING[face ^ 1].index(which)
@@ -168,7 +182,7 @@
             if x_mask is not None:
                 face = 0 if cx == 1 else 1
                 k = LEAVING[face ^ 1].index(which)
-                at = X_ROW + 10 * face + 2 * k
+                at = X_ROW + 10 * (face ^ 1) + 2 * k
                 pair = planes[at : at + 2, :]
                 upper, lower = pair[0:1], pair[1:2]
                 if cy == 1:
@@ -298,7 +312,7 @@
 
 
 def kernel(
-    sizes, pop, plan_in, out, ids, raw, plan, theirs, state, cube, packets, gone, interface_out, first, interface, planes, post, halo,
+    sizes, pop, plan_in, out, ids, raw, plan, theirs, state, cube, packets, gone, interface_out, first, interface, planes, corner, post, halo,
     load_sem, send_sem, recv_sem, answer_sem, near_sem, across_sem,
 ):
     ny, nz, total = sizes
@@ -398,7 +412,7 @@
     for b in range(4):
         unpacked(raw, cube, b)
 
-    pack_faces(cube, packets, 0, 4)
+    pack_faces(cube, packets, 0, 4, corner)
 
     @pl.when(even)
     def _():
@@ -408,14 +422,21 @@
     def _():
         pl.semaphore_wait(across_sem, 1)
 
+    gz = lax.rem(me, nz)
+    far_later = (gz == nz // 2 - 1) | (gz == nz - 1)
+    far_before = (gz == nz // 2) | (gz == 0)
+    early = (far_later | far_before) & (gz < nz // 2) & (lax.rem(me // nz, ny) // 2 < ny // 4)
     halos = []
     for b in range(4):
         if b > 0:
-            pack_faces(cube, packets, b, 4 + b)
-        for number, at, device in ((4 + b, b, later), (8 + b, 8 + b, before)):
+            pack_faces(cube, packets, b, 4 + b, corner)
+        for number, at, device, far in ((4 + b, b, later, far_later), (8 + b, 8 + b, before, far_before)):
             copy = remote(packets.at[4 + b], packets.at[at], number, device)
-            copy.start()
-            halos.append(copy)
+            pl.when(far)(copy.start)
+            halos.append((copy, far))
+    for copy, far in halos:
+        pl.when(jnp.logical_not(far))(copy.start)
+
     low = jnp.minimum(moved[0], moved[1])
     high = jnp.maximum(moved[0], moved[1])
     stay0 = jnp.where(low > 0, 0, jnp.where(high > 1, 1, 2))
@@ -435,35 +456,49 @@
 
     lax.fori_loop(0, 2, keep, 0)
 
-    for copy in halos:
+    orders.wait_recv()
+
+    def shear_of(j):
+        came = theirs[4, jnp.clip(theirs[5, jnp.clip(j - 2, 0, 1)], 0, 3)]
+        count = jnp.where(j == 0, plan[4, stay0], jnp.where(j == 1, plan[4, stay1], came))
+        return 1.0 / (jnp.full((8, 128), count, jnp.int32).astype(jnp.float32) * (1.0 / 1.6 - 0.5) + 0.5)
+
+    def start_foreign():
+        for copy in blocks:
+            copy.wait_recv()
+
+        def one(j, carry):
+            collide_first(first.at[j], post.at[j, 0], shear_of(j))
+            return carry
+
+        lax.fori_loop(2, 4, one, 0)
+
+    pl.when(early)(start_foreign)
+
+    for copy, _ in halos:
         copy.wait_recv()
 
     lowest = (me - 1) * 4
     faces = []
     for k in range(2):
-        assemble(packets, plan, moved[k], lowest, interface_out, k, moved[k])
+        assemble(packets, plan, moved[k], lowest, interface_out, k)
         copy = remote(interface_out.at[k], interface.at[2 + k], 2 + k, partner)
         copy.start()
         faces.append(copy)
 
     for j, stay in enumerate((stay0, stay1)):
-        assemble(packets, plan, stay, lowest, interface, j, stay)
+        assemble(packets, plan, stay, lowest, interface, j)
 
     def job(j, carry):
         for k in range(2):
             @pl.when(j == 2 + k)
             def _(k=k):
                 faces[k].wait_recv()
-                blocks[k].wait_recv()
-
-        count = jnp.broadcast_to(interface[j, COUNT_ROW : COUNT_ROW + 1, :], (8, 128))
-        shear = 1.0 / (count * (1.0 / 1.6 - 0.5) + 0.5)
+
+        pl.when((j == 2) & jnp.logical_not(early))(start_foreign)
+        shear = shear_of(j)
         spread(interface, j, planes)
         build_halo(planes, halo)
-
-        @pl.when(j >= 2)
-        def _():
-            collide_first(first.at[j], post.at[j, 0], shear)
 
         def one(step, inner_carry):
             now = lax.rem(step, 2)
@@ -476,7 +511,6 @@
 
     lax.fori_loop(0, 4, job, 0)
 
-    orders.wait_recv()
     for s in range(4):
         here = jnp.where(moved[0] == s, 2, jnp.where(moved[1] == s, 3, jnp.where(stay0 == s, 0, 1)))
         sent = jnp.where(moved[0] == s, theirs[5, 0], theirs[5, 1])
@@ -488,12 +522,15 @@
                 out[q, pl.ds(32 * v + s, 8, stride=4), :] = state[step, here, q, 8 * v : 8 * v + 8, :]
         ids[s] = jnp.where(foreign, partner_id * 4 + sent, me * 4 + s)
 
-    for copy in halos + blocks + faces + [orders]:
+    for copy in [copy for copy, _ in halos] + blocks + faces + [orders]:
         copy.wait_send()
 
 
 def write(result, ids_in, out, ids, sems):
-    copies = [pltpu.make_async_copy(result, out, sems.at[0]), pltpu.make_async_copy(ids_in, ids, sems.at[1])]
+    copies = [pltpu.make_async_copy(ids_in, ids, sems.at[4])]
+    for k, (low, count) in enumerate(((0, 5), (5, 5), (10, 5), (15, 4))):
+        part = pl.ds(low, count)
+        copies.append(pltpu.make_async_copy(result.at[part], out.at[part], sems.at[k]))
     for copy in copies:
         copy.start()
     for copy in copies:
@@ -526,6 +563,7 @@
             pltpu.VMEM((4, 19, 32, 128), f32),
             pltpu.VMEM((4, SENT_ROWS, 128), f32),
             pltpu.VMEM((PLANE_ROWS, 128), f32),
+            pltpu.VMEM((8, 128), f32),
             pltpu.VMEM((4, 2, 19, 48, 128), f32),
             pltpu.VMEM((19, 32, 128), f32),
             pltpu.SemaphoreType.DMA((2,)),
@@ -545,7 +583,7 @@
         out_shape=shapes,
         in_specs=[vmem, whole],
         out_specs=(whole, whole),
-        scratch_shapes=[pltpu.SemaphoreType.DMA((2,))],
+        scratch_shapes=[pltpu.SemaphoreType.DMA((5,))],
         compiler_params=pltpu.CompilerParams(vmem_limit_bytes=36 * 1024 * 1024),
         name="write_out",
     )(result, ids)

time: 30.7 us -> 29.7 us (0.967)
  Pallas kernels: 29.2 us -> 28.2 us
    pallas_call x1, Pallas kernels: 28.1 us -> 27.2 us  [shards(): pl.pallas_call(functools.partial(kernel, sizes), out_shape=shapes, in_spe...]
where the time goes in v4:
time: 29.7 us; the launch traced here: 29.6 us
  Pallas kernels  28.2 us (95%)
  other arithmetic  0.72 us (2%)
  between operations  0.64 us (2%)
    pallas_call x1, Pallas kernels, shards(): pl.pallas_call(functools.partial(kernel, sizes), out_shape=shapes, in_spe...  27.2 us
    pallas_call x1, Pallas kernels, shards(): pl.pallas_call(write, out_shape=shapes, in_specs=[vmem, whole], out_specs...  1.07 us
    concatenate x1, other arithmetic, shards(): jnp.concatenate([neighbours, jnp.pad(substeps[None], ((0, 0), (0, 2))), j...  0.72 us

profile of v4, /device:TPU:32, one launch (start us, length us, event | category | flops | bytes accessed | tf_op | source)
XLA Modules:
  0.0 29.6 jit_solution(13474622252641207527)
XLA Ops:
  0.6 0.7 %pad_add_fusion.plan_in = s32[6,6]{1,0:T(8,128)S(1)} fusion(s32[1,2]{1,0:T(1,128)} %param.7, s32[1,4]{1,0:T(1,128)} %bitcast.12, s32[4,6]{1,0:T(4,128)} %param.5), kind=kLoop, calls=%fused_computation | loop fusion | flops 72 | bytes 264 | tf_op jit(solution)/shard_map/concatenate | solution.py:543
  1.4 27.2 %lattice_step.1 = (f32[19,128,128]{2,1,0:T(8,128)S(1)}, s32[4]{0:T(128)S(1)}) custom-call(f32[19,128,128]{2,1,0:T(8,128)} %bitcast.11, s32[6,6]{1,0:T(8,128)S(1)} %pad_add_fusion.plan_in), custom_call_target="tpu_custom_call" | custom-call | tf_op jit(solution)/shard_map/lattice_step/pallas_call | solution.py:549
  28.5 1.1 %write_out.1 = (f32[19,128,128]{2,1,0:T(8,128)}, s32[4]{0:T(128)}) custom-call(f32[19,128,128]{2,1,0:T(8,128)S(1)} %get-tuple-element.6.result, s32[4]{0:T(128)S(1)} %get-tuple-element.7.ids_in), custom_call_target="tpu_custom_call" | custom-call | tf_op jit(solution)/shard_map/write_out/pallas_call | solution.py:581

commit v5 on v4

--- a/solution.py
+++ b/solution.py
@@ -106,11 +106,11 @@
     planes[X_ROW + 16 : X_ROW + 20, :] = jnp.where(lane < 64, rest, below)[0:4]
 
 
-def assemble(packets, plan, block, first, out, slot):
+def assemble(packets, nbr, block, first, out, slot):
     row, lane = grid_iotas()
     at, valid = [], []
     for face in range(6):
-        near = plan[block, face]
+        near = nbr[block, face]
         valid.append(jnp.full((8, 128), near, jnp.int32) >= 0)
         at.append(jnp.clip(near - first, 0, 11))
     place = (lane // 16 - row % 2) % 8
@@ -312,7 +312,7 @@
 
 
 def kernel(
-    sizes, pop, plan_in, out, ids, raw, plan, theirs, state, cube, packets, gone, interface_out, first, interface, planes, corner, post, halo,
+    sizes, pop, nbr_in, sub_in, moves_in, out, ids, raw, nbr, sub, moves, mine, theirs, state, cube, packets, gone, interface_out, first, interface, planes, corner, post, halo,
     load_sem, send_sem, recv_sem, answer_sem, near_sem, across_sem,
 ):
     ny, nz, total = sizes
@@ -328,7 +328,7 @@
     before = place(lax.rem(me + total - 1, total))
 
     loads = [
-        pltpu.make_async_copy(source, target, load_sem.at[k]) for k, (source, target) in enumerate(((plan_in, plan), (pop, raw)))
+        pltpu.make_async_copy(source, target, load_sem.at[k]) for k, (source, target) in enumerate(((pop, raw), (nbr_in, nbr), (sub_in, sub), (moves_in, moves)))
     ]
     for load in loads:
         load.start()
@@ -350,9 +350,9 @@
     def _():
         signal(barrier, before)
 
-    @pl.when(even & at_end)
-    def _():
-        signal(barrier, later)
+    @pl.when(odd & at_start)
+    def _():
+        signal(barrier, before)
 
     def remote(source, target, number, device):
         return pltpu.make_async_remote_copy(
@@ -364,9 +364,17 @@
             device_id_type=MESH,
         )
 
+    @pl.when(even & jnp.logical_not(at_end))
+    def _():
+        pl.semaphore_wait(barrier, 1)
+
+    @pl.when(even & at_end)
+    def _():
+        pl.semaphore_wait(barrier, 2)
+        signal(across_sem, later)
+
     @pl.when(even)
     def _():
-        pl.semaphore_wait(barrier, 1)
         signal(answer_sem, partner)
 
     @pl.when(odd)
@@ -380,59 +388,72 @@
     @pl.when(odd & jnp.logical_not(at_end))
     def _():
         signal(barrier, later)
+
+    gz = lax.rem(me, nz)
+    z_low = lax.rem(me // nz, ny) // 2
+    lowest_chips = z_low < ny // 4
+    late = gz >= nz // 2
+
+    def hear():
+        @pl.when(odd & jnp.logical_not(at_start))
+        def _():
+            pl.semaphore_wait(barrier, 2)
+
+        @pl.when(odd & at_start)
+        def _():
+            pl.semaphore_wait(barrier, 1)
+
+        @pl.when(odd)
+        def _():
+            signal(near_sem, partner)
+
+        @pl.when(odd & at_end)
+        def _():
+            signal(across_sem, later)
+
 
     for load in loads:
         load.wait()
 
-    moved = [plan[5, 0], plan[5, 1]]
+    moved = [moves[0, 0], moves[0, 1]]
+    for k in range(4):
+        mine[0, k] = sub[k]
+        mine[1, k] = moves[0, k % 2]
+    orders = remote(mine, theirs, 12, partner)
+    orders.start()
+    blocks = [remote(gone.at[k], first.at[2 + k], k, partner) for k in range(2)]
     for k in range(2):
         for q in range(19):
             for v in range(4):
                 gone[k, q, 8 * v : 8 * v + 8, :] = raw[q, pl.ds(32 * v + moved[k], 8, stride=4), :]
-
-    orders = remote(plan, theirs, 12, partner)
-    orders.start()
-    blocks = [remote(gone.at[k], first.at[2 + k], k, partner) for k in range(2)]
-    for copy in blocks:
-        copy.start()
-
-    @pl.when(odd)
-    def _():
-        pl.semaphore_wait(barrier, 2)
-        signal(near_sem, partner)
-
-    @pl.when(odd & at_start)
-    def _():
-        signal(across_sem, before)
-
-    @pl.when(odd & at_end)
-    def _():
-        signal(across_sem, later)
+        blocks[k].start()
 
     for b in range(4):
         unpacked(raw, cube, b)
 
+    hear()
+
     pack_faces(cube, packets, 0, 4, corner)
 
     @pl.when(even)
     def _():
         pl.semaphore_wait(near_sem, 1)
 
-    @pl.when(even & (at_start | at_end))
+    @pl.when(at_start)
     def _():
         pl.semaphore_wait(across_sem, 1)
 
-    gz = lax.rem(me, nz)
     far_later = (gz == nz // 2 - 1) | (gz == nz - 1)
     far_before = (gz == nz // 2) | (gz == 0)
-    early = (far_later | far_before) & (gz < nz // 2) & (lax.rem(me // nz, ny) // 2 < ny // 4)
+    early = (far_later | far_before) & jnp.logical_not(late) & lowest_chips
+    urgent = lowest_chips | at_end | jnp.logical_not(late)
     halos = []
     for b in range(4):
         if b > 0:
             pack_faces(cube, packets, b, 4 + b, corner)
         for number, at, device, far in ((4 + b, b, later, far_later), (8 + b, 8 + b, before, far_before)):
             copy = remote(packets.at[4 + b], packets.at[at], number, device)
-            pl.when(far)(copy.start)
+            pl.when(far & urgent)(copy.start)
             halos.append((copy, far))
     for copy, far in halos:
         pl.when(jnp.logical_not(far))(copy.start)
@@ -450,17 +471,20 @@
             return inner_carry
 
         lax.fori_loop(0, 19, one, 0)
-        count = jnp.full((8, 128), plan[4, stay], jnp.int32).astype(jnp.float32)
+        count = jnp.full((8, 128), sub[stay], jnp.int32).astype(jnp.float32)
         collide_first(first.at[j], post.at[j, 0], 1.0 / (count * (1.0 / 1.6 - 0.5) + 0.5))
         return carry
 
     lax.fori_loop(0, 2, keep, 0)
 
+    for copy, far in halos:
+        pl.when(far & jnp.logical_not(urgent))(copy.start)
+
     orders.wait_recv()
 
     def shear_of(j):
-        came = theirs[4, jnp.clip(theirs[5, jnp.clip(j - 2, 0, 1)], 0, 3)]
-        count = jnp.where(j == 0, plan[4, stay0], jnp.where(j == 1, plan[4, stay1], came))
+        came = theirs[0, jnp.clip(theirs[1, jnp.clip(j - 2, 0, 1)], 0, 3)]
+        count = jnp.where(j == 0, sub[stay0], jnp.where(j == 1, sub[stay1], came))
         return 1.0 / (jnp.full((8, 128), count, jnp.int32).astype(jnp.float32) * (1.0 / 1.6 - 0.5) + 0.5)
 
     def start_foreign():
@@ -481,13 +505,13 @@
     lowest = (me - 1) * 4
     faces = []
     for k in range(2):
-        assemble(packets, plan, moved[k], lowest, interface_out, k)
+        assemble(packets, nbr, moved[k], lowest, interface_out, k)
         copy = remote(interface_out.at[k], interface.at[2 + k], 2 + k, partner)
         copy.start()
         faces.append(copy)
 
     for j, stay in enumerate((stay0, stay1)):
-        assemble(packets, plan, stay, lowest, interface, j)
+        assemble(packets, nbr, stay, lowest, interface, j)
 
     def job(j, carry):
         for k in range(2):
@@ -513,9 +537,9 @@
 
     for s in range(4):
         here = jnp.where(moved[0] == s, 2, jnp.where(moved[1] == s, 3, jnp.where(stay0 == s, 0, 1)))
-        sent = jnp.where(moved[0] == s, theirs[5, 0], theirs[5, 1])
+        sent = jnp.where(moved[0] == s, theirs[1, 0], theirs[1, 1])
         foreign = here >= 2
-        count = jnp.where(foreign, theirs[4, jnp.clip(sent, 0, 3)], plan[4, s])
+        count = jnp.where(foreign, theirs[0, jnp.clip(sent, 0, 3)], sub[s])
         step = jnp.clip(count - 1, 0, 3)
         for q in range(19):
             for v in range(4):
@@ -540,21 +564,21 @@
 def shards(sizes, populations, neighbours, substeps, moves):
     f32 = jnp.float32
     lying = populations.reshape(4, 19, 32, 128).transpose(1, 2, 0, 3).reshape(19, 128, 128)
-    plan = jnp.concatenate(
-        [neighbours, jnp.pad(substeps[None], ((0, 0), (0, 2))), jnp.pad(moves, ((0, 0), (0, 4)))], axis=0
-    )
     vmem, smem = pl.BlockSpec(memory_space=pltpu.VMEM), pl.BlockSpec(memory_space=pltpu.SMEM)
     whole = pl.BlockSpec(memory_space=pl.ANY)
     shapes = (jax.ShapeDtypeStruct((19, 128, 128), f32), jax.ShapeDtypeStruct((4,), jnp.int32))
     result, ids = pl.pallas_call(
         functools.partial(kernel, sizes),
-        out_shape=shapes,
-        in_specs=[whole, whole],
+        out_shape=(pltpu.VMEM((19, 128, 128), f32), shapes[1]),
+        in_specs=[pl.BlockSpec(memory_space=pltpu.HBM)] * 4,
         out_specs=(vmem, smem),
         scratch_shapes=[
             pltpu.VMEM((19, 128, 128), f32),
-            pltpu.SMEM((6, 6), jnp.int32),
-            pltpu.SMEM((6, 6), jnp.int32),
+            pltpu.SMEM((4, 6), jnp.int32),
+            pltpu.SMEM((4,), jnp.int32),
+            pltpu.SMEM((1, 2), jnp.int32),
+            pltpu.SMEM((2, 4), jnp.int32),
+            pltpu.SMEM((2, 4), jnp.int32),
             pltpu.VMEM((4, 4, 19, 32, 128), f32),
             pltpu.VMEM((4, 19, 48, 128), f32),
             pltpu.VMEM((12, SENT_ROWS, 128), f32),
@@ -566,7 +590,7 @@
             pltpu.VMEM((8, 128), f32),
             pltpu.VMEM((4, 2, 19, 48, 128), f32),
             pltpu.VMEM((19, 32, 128), f32),
-            pltpu.SemaphoreType.DMA((2,)),
+            pltpu.SemaphoreType.DMA((4,)),
             pltpu.SemaphoreType.DMA((13,)),
             pltpu.SemaphoreType.DMA((13,)),
             pltpu.SemaphoreType.REGULAR,
@@ -577,7 +601,7 @@
             collective_id=0, has_side_effects=True, vmem_limit_bytes=53500 * 1024
         ),
         name="lattice_step",
-    )(lying, plan)
+    )(*[pltpu.with_memory_space_constraint(value, pltpu.HBM) for value in (lying, neighbours, substeps, moves)])
     result, ids = pl.pallas_call(
         write,
         out_shape=shapes,

time: 29.7 us -> 28.2 us (0.949)
  other arithmetic: 0.72 us -> 0 us
  Pallas kernels: 28.2 us -> 27.5 us
    pallas_call x1, Pallas kernels: 27.2 us -> 26.4 us  [shards(): pl.pallas_call(functools.partial(kernel, sizes), out_shape=(pltpu.VMEM((1...]
    concatenate x1 -> x0, other arithmetic: 0.72 us -> none  [shards(): jnp.concatenate([neighbours, jnp.pad(substeps[None], ((0, 0), (0, 2))), j...]
where the time goes in v5:
time: 28.2 us; the launch traced here: 28.1 us
  Pallas kernels  27.5 us (98%)
  between operations  0.64 us (2%)
    pallas_call x1, Pallas kernels, shards(): pl.pallas_call(functools.partial(kernel, sizes), out_shape=(pltpu.VMEM((1...  26.4 us
    pallas_call x1, Pallas kernels, shards(): pl.pallas_call(write, out_shape=shapes, in_specs=[vmem, whole], out_specs...  1.07 us

profile of v5, /device:TPU:32, one launch (start us, length us, event | category | flops | bytes accessed | tf_op | source)
XLA Modules:
  0.0 28.1 jit_solution(9605982634258578704)
XLA Ops:
  0.6 26.4 %lattice_step.1 = (f32[19,128,128]{2,1,0:T(8,128)S(1)}, s32[4]{0:T(128)S(1)}) custom-call(f32[19,128,128]{2,1,0:T(8,128)} %bitcast.10, s32[4,6]{1,0:T(4,128)} %nbr_in.1, s32[4]{0:T(128)} %sub_in.1, s32[1,2]{1,0:T(1,128)} %moves_in.1), custom_call_target="tpu_custom_call" | custom-call | tf_op jit(solution)/shard_map/lattice_step/pallas_call | solution.py:570
  27.1 1.1 %write_out.1 = (f32[19,128,128]{2,1,0:T(8,128)}, s32[4]{0:T(128)}) custom-call(f32[19,128,128]{2,1,0:T(8,128)S(1)} %get-tuple-element.6.result, s32[4]{0:T(128)S(1)} %get-tuple-element.7.ids_in), custom_call_target="tpu_custom_call" | custom-call | tf_op jit(solution)/shard_map/write_out/pallas_call | solution.py:605

commit v6 on v5

--- a/solution.py
+++ b/solution.py
@@ -333,24 +333,24 @@
     for load in loads:
         load.start()
 
-    odd = lax.rem(me // bit, 2) == 1
+    greeter = lax.rem(me // bit, 2) == 0
     inner = lax.rem(me, bit)
     at_start, at_end = inner == 0, inner == bit - 1
-    even = jnp.logical_not(odd)
+    answerer = jnp.logical_not(greeter)
     barrier = pltpu.get_barrier_semaphore()
 
     def signal(semaphore, device):
         pl.semaphore_signal(semaphore, inc=1, device_id=device, device_id_type=MESH)
 
-    @pl.when(odd)
+    @pl.when(greeter)
     def _():
         signal(barrier, partner)
 
-    @pl.when(even & at_start)
+    @pl.when(answerer & at_start)
     def _():
         signal(barrier, before)
 
-    @pl.when(odd & at_start)
+    @pl.when(greeter & at_start)
     def _():
         signal(barrier, before)
 
@@ -364,28 +364,28 @@
             device_id_type=MESH,
         )
 
-    @pl.when(even & jnp.logical_not(at_end))
+    @pl.when(answerer & jnp.logical_not(at_end))
     def _():
         pl.semaphore_wait(barrier, 1)
 
-    @pl.when(even & at_end)
+    @pl.when(answerer & at_end)
     def _():
         pl.semaphore_wait(barrier, 2)
         signal(across_sem, later)
 
-    @pl.when(even)
+    @pl.when(answerer)
     def _():
         signal(answer_sem, partner)
 
-    @pl.when(odd)
+    @pl.when(greeter)
     def _():
         pl.semaphore_wait(answer_sem, 1)
 
-    @pl.when(odd & jnp.logical_not(at_start))
+    @pl.when(greeter & jnp.logical_not(at_start))
     def _():
         signal(barrier, before)
 
-    @pl.when(odd & jnp.logical_not(at_end))
+    @pl.when(greeter & jnp.logical_not(at_end))
     def _():
         signal(barrier, later)
 
@@ -395,19 +395,19 @@
     late = gz >= nz // 2
 
     def hear():
-        @pl.when(odd & jnp.logical_not(at_start))
+        @pl.when(greeter & jnp.logical_not(at_start))
         def _():
             pl.semaphore_wait(barrier, 2)
 
-        @pl.when(odd & at_start)
+        @pl.when(greeter & at_start)
         def _():
             pl.semaphore_wait(barrier, 1)
 
-        @pl.when(odd)
+        @pl.when(greeter)
         def _():
             signal(near_sem, partner)
 
-        @pl.when(odd & at_end)
+        @pl.when(greeter & at_end)
         def _():
             signal(across_sem, later)
 
@@ -435,7 +435,7 @@
 
     pack_faces(cube, packets, 0, 4, corner)
 
-    @pl.when(even)
+    @pl.when(answerer)
     def _():
         pl.semaphore_wait(near_sem, 1)
 

time: 28.2 us -> 27.9 us (0.989)
  the two profiles are of different devices: /device:TPU:32 before, /device:TPU:30 now
where the time goes in v6:
time: 27.9 us; the launch traced here: 27.8 us
  Pallas kernels  27.2 us (97%)
  between operations  0.64 us (2%)
    pallas_call x1, Pallas kernels, shards(): pl.pallas_call(functools.partial(kernel, sizes), out_shape=(pltpu.VMEM((1...  26.1 us
    pallas_call x1, Pallas kernels, shards(): pl.pallas_call(write, out_shape=shapes, in_specs=[vmem, whole], out_specs...  1.07 us

profile of v6, /device:TPU:30, one launch (start us, length us, event | category | flops | bytes accessed | tf_op | source)
XLA Modules:
  0.0 27.8 jit_solution(17393251456703200047)
XLA Ops:
  0.6 26.1 %lattice_step.1 = (f32[19,128,128]{2,1,0:T(8,128)S(1)}, s32[4]{0:T(128)S(1)}) custom-call(f32[19,128,128]{2,1,0:T(8,128)} %bitcast.10, s32[4,6]{1,0:T(4,128)} %nbr_in.1, s32[4]{0:T(128)} %sub_in.1, s32[1,2]{1,0:T(1,128)} %moves_in.1), custom_call_target="tpu_custom_call" | custom-call | tf_op jit(solution)/shard_map/lattice_step/pallas_call | solution.py:570
  26.7 1.1 %write_out.1 = (f32[19,128,128]{2,1,0:T(8,128)}, s32[4]{0:T(128)}) custom-call(f32[19,128,128]{2,1,0:T(8,128)S(1)} %get-tuple-element.6.result, s32[4]{0:T(128)S(1)} %get-tuple-element.7.ids_in), custom_call_target="tpu_custom_call" | custom-call | tf_op jit(solution)/shard_map/write_out/pallas_call | solution.py:605

commit v7 on v6

--- a/solution.py
+++ b/solution.py
@@ -446,7 +446,7 @@
     far_later = (gz == nz // 2 - 1) | (gz == nz - 1)
     far_before = (gz == nz // 2) | (gz == 0)
     early = (far_later | far_before) & jnp.logical_not(late) & lowest_chips
-    urgent = lowest_chips | at_end | jnp.logical_not(late)
+    urgent = lowest_chips | at_end | jnp.logical_not(late) | (gz == nz // 2)
     halos = []
     for b in range(4):
         if b > 0:

time: 27.9 us -> 27.9 us (level)
  no operation moved by 1% of the time
where the time goes in v7:
time: 27.9 us; the launch traced here: 27.8 us
  Pallas kernels  27.2 us (97%)
  between operations  0.64 us (2%)
    pallas_call x1, Pallas kernels, shards(): pl.pallas_call(functools.partial(kernel, sizes), out_shape=(pltpu.VMEM((1...  26.1 us
    pallas_call x1, Pallas kernels, shards(): pl.pallas_call(write, out_shape=shapes, in_specs=[vmem, whole], out_specs...  1.07 us

profile of v7, /device:TPU:30, one launch (start us, length us, event | category | flops | bytes accessed | tf_op | source)
XLA Modules:
  0.0 27.8 jit_solution(17309834881598027873)
XLA Ops:
  0.6 26.1 %lattice_step.1 = (f32[19,128,128]{2,1,0:T(8,128)S(1)}, s32[4]{0:T(128)S(1)}) custom-call(f32[19,128,128]{2,1,0:T(8,128)} %bitcast.10, s32[4,6]{1,0:T(4,128)} %nbr_in.1, s32[4]{0:T(128)} %sub_in.1, s32[1,2]{1,0:T(1,128)} %moves_in.1), custom_call_target="tpu_custom_call" | custom-call | tf_op jit(solution)/shard_map/lattice_step/pallas_call | solution.py:570
  26.7 1.1 %write_out.1 = (f32[19,128,128]{2,1,0:T(8,128)}, s32[4]{0:T(128)}) custom-call(f32[19,128,128]{2,1,0:T(8,128)S(1)} %get-tuple-element.6.result, s32[4]{0:T(128)S(1)} %get-tuple-element.7.ids_in), custom_call_target="tpu_custom_call" | custom-call | tf_op jit(solution)/shard_map/write_out/pallas_call | solution.py:605
